TPU v7x, 256 devices: a whole 4x4x8 slice. The times are simulated.
256 devices in a mesh: mem: 8 (over x, y_lo), tile: 32 (over z, y_hi, core).
Axes of the slice: x: 4, y: 4 (y_hi: 2, y_lo: 2; y = y_hi * 2 + y_lo), z: 8, core: 2. Of those that a mesh axis runs over, the one named last changes fastest.
Arguments:
- ensemble: bfloat16 [64, 72, 512, 128], P('mem', None, 'tile'), may hold values from -6 to 6
- weights: bfloat16 [1024, 64, 64], P('tile'), may hold values from -0.75 to 0.75
- patch_index: int32 [512, 128], P('tile'), may hold values from 0 to 31
- courant: float32 [2, 72, 512, 128], P(None, None, 'tile'), may hold values from -0.95 to 0.95
- vert_inverse: bfloat16 [512, 72, 72], P('tile'), may hold values from -0.23570226 to 1.2357023
Outputs:
- forecast: bfloat16 [64, 72, 512, 128], P('mem', None, 'tile')
All inputs are finite; a program needn't handle non-finite values.
Results may differ from a plain program's by a relative error of at most 0.0078.
Values may be sent and summed in bfloat16 or wider, within the bound.
No kernel may reach another device: no remote copies, remote signals or barrier semaphores. Data moves between devices by JAX's collectives and lax.ppermute only.
A program may use at most 192 MiB of HBM per device.

v0:
```python
import functools

import jax
import jax.numpy as jnp
from jax import lax
from jax.experimental import pallas as pl
from jax.experimental.pallas import tpu as pltpu
from jax.sharding import PartitionSpec as P

ROUNDS = (3, 3)
GROUPS = 2
LEVELS = 72
PAIR = 2 * LEVELS
TILE_ROWS = 16
WEIGHT_ROWS = LEVELS + 8
LANES = 128


def stencil_weights(numbers):
    location = -jnp.abs(numbers)
    far = -(location + 1.0) * location * (location - 1.0) / 6.0
    near = (location + 2.0) * location * (location - 1.0) / 2.0
    mid = -(location + 2.0) * (location + 1.0) * (location - 1.0) / 2.0
    ahead = (location + 2.0) * (location + 1.0) * location / 6.0
    forward = numbers >= 0.0
    zero = jnp.zeros_like(far)
    return [
        jnp.where(forward, far, zero),
        jnp.where(forward, near, ahead),
        mid,
        jnp.where(forward, ahead, near),
        jnp.where(forward, zero, far),
    ]


def column_weights(numbers):
    numbers = jnp.transpose(numbers, (2, 0, 1, 3))
    lon = stencil_weights(numbers[:, 0])
    lat = stencil_weights(numbers[:, 1])
    row = lax.broadcasted_iota(jnp.int32, lat[0].shape, 2)
    last = LANES - 1
    inside = [row >= 2, row >= 1, row >= 0, row <= last - 1, row <= last - 2]
    lat = [jnp.where(keep, weight, 0.0) for keep, weight in zip(inside, lat)]
    both = jnp.stack(lon + lat, axis=1)
    return jnp.concatenate([both, both[:, :, :8]], axis=2)


def weighted(values, weights):
    total = values[0] * weights[0]
    for value, weight in zip(values[1:], weights[1:]):
        total = total + value * weight
    return total


def advect_kernel(steps, rows, before, owned, after, weights, inverse, out, field, other, across_0, across_1,
                  weight, operator, field_sem, weight_sem, operator_sem):
    halo = 2 * steps
    length = owned.shape[0]
    computed = weight.shape[0]
    first = (computed - (length + 4 * (steps - 1))) // 2
    parts = ((before, 0, halo), (owned, halo, length), (after, halo + length, halo))
    loads = [pltpu.make_async_copy(ref, field.at[pl.ds(at, count)], field_sem.at[index])
             for index, (ref, at, count) in enumerate(parts)]
    loads.append(pltpu.make_async_copy(inverse, operator, operator_sem))
    for load in loads:
        load.start()

    def weight_load(column):
        return pltpu.make_async_copy(weights.at[column], weight.at[column], weight_sem.at[column])

    def start_load(column, carry):
        weight_load(column).start()
        return carry

    lax.fori_loop(first, computed - first, start_load, 0)
    for load in loads:
        load.wait()

    pairs = rows // PAIR

    def stencils(source, column, w_column, across):
        for tile in range(PAIR // TILE_ROWS):
            level = (tile * TILE_ROWS) % LEVELS
            w = [weight[w_column, k, pl.ds(level, TILE_ROWS), :] for k in range(10)]
            for pair in range(pairs):
                at = pl.ds(pair * PAIR + tile * TILE_ROWS, TILE_ROWS)
                values = [source[column + k, at, :].astype(jnp.float32) for k in range(5)]
                along = weighted(values, w[:5])
                shifted = [pltpu.roll(along, 2, 1), pltpu.roll(along, 1, 1), along,
                           pltpu.roll(along, LANES - 1, 1), pltpu.roll(along, LANES - 2, 1)]
                across[at, :] = weighted(shifted, w[5:]).astype(jnp.bfloat16)

    def vertical(across, target, column, w_column):
        side = jnp.concatenate([across[pl.ds(pair * PAIR, PAIR), :] for pair in range(pairs)], axis=1)
        mixed = jnp.dot(operator[w_column], side, preferred_element_type=jnp.float32).astype(jnp.bfloat16)
        for pair in range(pairs):
            target[column, pl.ds(pair * PAIR, PAIR), :] = mixed[:, pair * LANES:(pair + 1) * LANES]

    buffers = (field, other)
    for step in range(steps):
        source = buffers[step % 2]
        target = out if step == steps - 1 else buffers[(step + 1) % 2]
        columns = length + 4 * (steps - 1 - step)
        shift = first + 2 * step

        def arrive(column):
            if step == 0:
                weight_load(column).wait()

        arrive(shift)
        stencils(source, 0, shift, across_0)

        def pair_of_columns(index, carry):
            even = 2 * index
            arrive(shift + even + 1)
            vertical(across_0, target, even, shift + even)
            stencils(source, even + 1, shift + even + 1, across_1)
            arrive(shift + even + 2)
            vertical(across_1, target, even + 1, shift + even + 1)
            stencils(source, even + 2, shift + even + 2, across_0)
            return carry

        lax.fori_loop(0, columns // 2 - 1, pair_of_columns, 0)
        even = columns - 2
        arrive(shift + even + 1)
        vertical(across_0, target, even, shift + even)
        stencils(source, even + 1, shift + even + 1, across_1)
        vertical(across_1, target, even + 1, shift + even + 1)


def advect(steps, before, owned, after, weights, inverse):
    length, rows, lanes = owned.shape
    computed = weights.shape[0]
    anywhere = pl.BlockSpec(memory_space=pl.ANY)
    work = (length + 2 * steps) * steps * rows * lanes
    return pl.pallas_call(
        functools.partial(advect_kernel, steps, rows),
        out_shape=jax.ShapeDtypeStruct(owned.shape, owned.dtype),
        in_specs=[anywhere] * 5,
        out_specs=pl.BlockSpec(memory_space=pltpu.VMEM),
        scratch_shapes=[
            pltpu.VMEM((length + 4 * steps, rows, lanes), jnp.bfloat16),
            pltpu.VMEM((length + 4 * steps, rows, lanes), jnp.bfloat16),
            pltpu.VMEM((rows, lanes), jnp.bfloat16),
            pltpu.VMEM((rows, lanes), jnp.bfloat16),
            pltpu.VMEM(weights.shape, jnp.float32),
            pltpu.VMEM(inverse.shape, jnp.bfloat16),
            pltpu.SemaphoreType.DMA((3,)),
            pltpu.SemaphoreType.DMA((computed,)),
            pltpu.SemaphoreType.DMA,
        ],
        compiler_params=pltpu.CompilerParams(vmem_limit_bytes=30 * 1024 * 1024),
        cost_estimate=pl.CostEstimate(flops=work * (2 * LEVELS + 20), bytes_accessed=weights.size * 4, transcendentals=0),
    )(before, owned, after, weights, inverse)


def from_sides(array, width, dim):
    peers, length = lax.axis_size("tile"), array.shape[dim]
    up = [(i, (i + 1) % peers) for i in range(peers)]
    down = [(j, i) for i, j in up]
    before = lax.ppermute(lax.slice_in_dim(array, length - width, length, axis=dim), "tile", up)
    after = lax.ppermute(lax.slice_in_dim(array, 0, width, axis=dim), "tile", down)
    return before, after


def extended(array, width, dim):
    before, after = from_sides(array, width, dim)
    return jnp.concatenate([before, array, after], axis=dim)


def shards(ensemble, weights, patch_index, courant, vert_inverse):
    peers = lax.axis_size("mem")
    members, levels, length, lanes = ensemble.shape
    share = length // peers
    margin = 2 * (max(ROUNDS) - 1)

    to_send = jnp.transpose(ensemble, (2, 0, 1, 3)).reshape(peers, share, members, levels, lanes)
    arrived = lax.all_to_all(to_send, "mem", split_axis=0, concat_axis=0, tiled=True)

    patches = lax.dynamic_slice_in_dim(patch_index, lax.axis_index("mem") * share, share, 0)
    chosen = jnp.take(weights, patches, axis=0)
    numbers = column_weights(extended(courant, margin, 2))
    inverse = extended(vert_inverse, margin, 0)
    empty = jnp.zeros_like(inverse)
    inverse = jnp.concatenate([jnp.concatenate([inverse, empty], 2), jnp.concatenate([empty, inverse], 2)], 1)

    blended = jnp.einsum("ijco,iclj->iolj", chosen,
                         jnp.transpose(arrived, (1, 0, 2, 3, 4)).reshape(share, -1, levels, lanes),
                         preferred_element_type=jnp.float32).astype(jnp.bfloat16)
    blended = jnp.transpose(blended.reshape(share, peers, members, levels, lanes), (1, 0, 2, 3, 4))
    analysed = lax.all_to_all(blended, "mem", split_axis=0, concat_axis=0, tiled=True)
    fields = analysed.reshape(length, GROUPS, -1, lanes)
    fields = [fields[:, group] for group in range(GROUPS)]
    for steps in ROUNDS:
        sides = [from_sides(field, 2 * steps, 0) for field in fields]
        fields = [advect(steps, before, field, after, numbers, inverse)
                  for field, (before, after) in zip(fields, sides)]
    forecast = jnp.stack(fields, axis=1).reshape(length, members, levels, lanes)
    return jnp.transpose(forecast, (1, 2, 0, 3))


def solution(mesh):
    return jax.shard_map(
        shards,
        mesh=mesh,
        in_specs=(
            P("mem", None, "tile", None),
            P("tile", None, None),
            P("tile", None),
            P(None, None, "tile", None),
            P("tile", None, None),
        ),
        out_specs=P("mem", None, "tile", None),
        check_vma=False,
    )
```

profile of v0, /device:TPU:128, one launch (start us, length us, event | category | flops | bytes accessed | tf_op | source)
XLA Modules:
  0.0 217.0 jit_solution(2105532065445219732)
XLA Ops:
  0.0 1.8 copy.32
  2.0 5.3 %collective-permute-start.3 = (f32[2,72,4,128]{3,1,0,2:T(8,128)S(1)}, f32[2,72,4,128]{3,1,0,2:T(8,128)}, u32[]{:S(2)}, u32[]{:S(2)}) collective-permute-start(f32[2,72,4,128]{3,1,0,2:T(8,128)S(1)} %get-tuple-element.20), channel_id=1, source_target_pairs={{1,0},{2,1},{3,2},{4,3},{5,4},{6,5},{7,6},{8,7},{9,8},{10,9},{11,1... | collective-permute-start | bytes 884744 | tf_op jit(solution)/shard_map/ppermute | solution.py:162
  7.3 2.0 copy.26
  9.3 5.4 %all-to-all-start = ((bf16[8,2,8,72,128]{4,3,2,1,0:T(8,128)(2,1)}), bf16[8,2,8,72,128]{4,3,2,1,0:T(8,128)(2,1)}, u32[]{:S(2)}, u32[]{:S(2)}) async-start(bf16[8,2,8,72,128]{4,3,2,1,0:T(8,128)(2,1)} %bitcast.52), calls=%async_computation | async-start | bytes 4718592 | tf_op jit(solution)/shard_map/all_to_all | solution.py:178
  14.9 5.3 %collective-permute-start.5 = (bf16[4,72,72]{2,1,0:T(8,128)(2,1)S(1)}, bf16[4,72,72]{2,1,0:T(8,128)(2,1)S(1)}, u32[]{:S(2)}, u32[]{:S(2)}) collective-permute-start(bf16[4,72,72]{2,1,0:T(8,128)(2,1)S(1)} %get-tuple-element.21), channel_id=1, source_target_pairs={{1,0},{2,1},{3,2},{4,3},{5,4},{6,5},{7,6},{8,7},{9,8},{10,9},{11,1... | collective-permute-start | bytes 124424 | tf_op jit(solution)/shard_map/ppermute | solution.py:162
  22.2 3.1 %gather_fusion = bf16[256,64,64]{2,1,0:T(8,128)(2,1)} fusion(bf16[32,64,64]{2,1,0:T(8,128)(2,1)S(1)} %copy-done, s32[1024]{0:T(1024)S(1)} %pad_clamp_fusion), kind=kCustom, calls=%fused_computation | custom fusion | bytes 4195328 | tf_op jit(solution)/shard_map/jit(_take)/gather | solution.py:181
  25.3 6.4 %copy.25 = bf16[2,128,64,64]{2,3,1,0:T(8,128)(2,1)} copy(bf16[2,128,64,64]{3,2,1,0:T(8,128)(2,1)} %bitcast.50) | data formatting | bytes 4194304 | tf_op jit(solution)/shard_map/jit(_take)/gather | solution.py:181
  34.2 1.3 select_dynamic-update-slice_fusion.7
  36.2 1.4 select_dynamic-update-slice_fusion.6
  37.6 8.8 %all-to-all-done = bf16[8,2,8,72,128]{4,3,2,1,0:T(8,128)(2,1)} async-done(((bf16[8,2,8,72,128]{4,3,2,1,0:T(8,128)(2,1)}), bf16[8,2,8,72,128]{4,3,2,1,0:T(8,128)(2,1)}, u32[]{:S(2)}, u32[]{:S(2)}) %all-to-all-start) | async-done | bytes 2359328 | tf_op jit(solution)/shard_map/all_to_all | solution.py:178
  46.4 6.3 %copy.27 = bf16[2,8,8,72,128]{3,2,1,4,0:T(8,128)(2,1)} copy(bf16[2,8,8,72,128]{4,3,2,0,1:T(8,128)(2,1)} %bitcast.4) | data formatting | bytes 4718592 | tf_op jit(solution)/shard_map/transpose | solution.py:188
  52.7 6.8 %convert_bitcast_fusion = bf16[2,8,8,72,128]{3,2,1,4,0:T(8,128)(2,1)} fusion(bf16[2,8,8,72,128]{3,2,1,4,0:T(8,128)(2,1)} %copy.27, bf16[2,128,64,64]{2,3,1,0:T(8,128)(2,1)} %copy.25, pred[2,128]{1,0:T(4,128)(4,1)S(1)} %compare_and_fusion), kind=kOutput, calls=%fused_computation.4 | convolution fusion | flops 153223168 | bytes 6816000 | tf_op jit(solution)/shard_map/ijco,iclj->iolj/dot_general | solution.py:187
  59.4 6.3 %copy.28 = bf16[2,8,8,72,128]{4,3,2,0,1:T(8,128)(2,1)} copy(bf16[2,8,8,72,128]{3,2,1,4,0:T(8,128)(2,1)} %convert_bitcast_fusion) | data formatting | bytes 4718592 | tf_op jit(solution)/shard_map/reshape | solution.py:190
  65.7 4.6 %all-to-all-start.1 = ((bf16[8,2,8,72,128]{4,3,2,1,0:T(8,128)(2,1)}), bf16[8,2,8,72,128]{4,3,2,1,0:T(8,128)(2,1)}, u32[]{:S(2)}, u32[]{:S(2)}) async-start(bf16[8,2,8,72,128]{4,3,2,1,0:T(8,128)(2,1)} %bitcast.51), calls=%async_computation.1 | async-start | bytes 4718592 | tf_op jit(solution)/shard_map/all_to_all | solution.py:191
  71.5 2.3 %select_dynamic-update-slice_fusion.5 = f32[24,10,72,128]{3,2,1,0:T(8,128)} fusion(f32[24,10,72,128]{3,2,1,0:T(8,128)} %fusion.20, pred[24,1,72,128]{3,2,1,0:T(8,128)(4,1)} %copy-done.4, f32[24,2,72,128]{3,2,1,0:T(8,128)S(1)} %maximum_bitcast_fusion), kind=kLoop, calls=%fused_computation.45 | loop fusion | flops 2654208 | bytes 1990656
  75.1 1.4 select_dynamic-update-slice_fusion.3
  76.4 1.4 select_dynamic-update-slice_fusion.2
  79.0 1.4 select_dynamic-update-slice_fusion.1
  80.4 1.3 select_dynamic-update-slice_fusion
  83.0 22.7 %all-to-all-done.1 = bf16[8,2,8,72,128]{4,3,2,1,0:T(8,128)(2,1)} async-done(((bf16[8,2,8,72,128]{4,3,2,1,0:T(8,128)(2,1)}), bf16[8,2,8,72,128]{4,3,2,1,0:T(8,128)(2,1)}, u32[]{:S(2)}, u32[]{:S(2)}) %all-to-all-start.1) | async-done | bytes 2359328 | tf_op jit(solution)/shard_map/all_to_all | solution.py:191
  105.7 1.5 slice_bitcast_fusion.4
  107.8 4.9 %collective-permute-start.1 = (bf16[6,288,128]{2,1,0:T(8,128)(2,1)S(1)}, bf16[6,288,128]{2,1,0:T(8,128)(2,1)S(1)}, u32[]{:S(2)}, u32[]{:S(2)}) collective-permute-start(bf16[6,288,128]{2,1,0:T(8,128)(2,1)S(1)} %get-tuple-element.9), channel_id=1, source_target_pairs={{1,0},{2,1},{3,2},{4,3},{5,4},{6,5},{7,6},{8,7},{9,8},{10,9},{11,1... | collective-permute-start | bytes 1327112 | tf_op jit(solution)/shard_map/ppermute | solution.py:162
  112.7 4.5 %pad_maximum_fusion.weights = f32[24,10,80,128]{3,2,1,0:T(8,128)S(1)} fusion(f32[24,10,8,128]{3,2,1,0:T(8,128)S(1)} %slice.97, f32[24,10,72,128]{3,2,1,0:T(8,128)} %select_dynamic-update-slice_fusion), kind=kLoop, calls=%fused_computation.1 | loop fusion | flops 2457600 | bytes 19660800 | tf_op jit(solution)/shard_map/concatenate | solution.py:45
  117.3 5.3 %collective-permute-start.9 = (bf16[6,288,128]{2,1,0:T(8,128)(2,1)S(1)}, bf16[6,288,128]{2,1,0:T(8,128)(2,1)S(1)}, u32[]{:S(2)}, u32[]{:S(2)}) collective-permute-start(bf16[6,288,128]{2,1,0:T(8,128)(2,1)S(1)} %get-tuple-element.12), channel_id=1, source_target_pairs={{1,0},{2,1},{3,2},{4,3},{5,4},{6,5},{7,6},{8,7},{9,8},{10,9},{11,1... | collective-permute-start | bytes 1327112 | tf_op jit(solution)/shard_map/ppermute | solution.py:162
  122.6 1.8 slice_bitcast_fusion.1
  124.5 19.5 %shard_map.55.owned = bf16[16,288,128]{2,1,0:T(8,128)(2,1)S(1)} custom-call(bf16[6,288,128]{2,1,0:T(8,128)(2,1)S(1)} %collective-permute-done.before, bf16[16,288,128]{2,1,0:T(8,128)(2,1)S(1)} %get-tuple-element.13.owned, bf16[6,288,128]{2,1,0:T(8,128)(2,1)S(1)} %collective-permute-done.1.after, f32[24,10,80,128]{3,2,1,0:T(8,128)S(1)} %pad_maximum_fusion.weights, ...), custom_call_target="tpu_custom_call" | custom-call | flops 399015936 | bytes 9830400 | tf_op jit(solution)/shard_map/pallas_call | solution.py:136
  144.1 5.3 %collective-permute-start.7 = (bf16[6,288,128]{2,1,0:T(8,128)(2,1)S(1)}, bf16[6,288,128]{2,1,0:T(8,128)(2,1)S(1)}, u32[]{:S(2)}, u32[]{:S(2)}) collective-permute-start(bf16[6,288,128]{2,1,0:T(8,128)(2,1)S(1)} %get-tuple-element.15), channel_id=1, source_target_pairs={{1,0},{2,1},{3,2},{4,3},{5,4},{6,5},{7,6},{8,7},{9,8},{10,9},{11,1... | collective-permute-start | bytes 1327112 | tf_op jit(solution)/shard_map/ppermute | solution.py:162
  149.5 19.5 %shard_map.57.owned = bf16[16,288,128]{2,1,0:T(8,128)(2,1)S(1)} custom-call(bf16[6,288,128]{2,1,0:T(8,128)(2,1)S(1)} %collective-permute-done.8.before, bf16[16,288,128]{2,1,0:T(8,128)(2,1)S(1)} %get-tuple-element.14.owned, bf16[6,288,128]{2,1,0:T(8,128)(2,1)S(1)} %collective-permute-done.9.after, f32[24,10,80,128]{3,2,1,0:T(8,128)S(1)} %pad_maximum_fusion.weights, ...), custom_call_target="tpu_custom_call" | custom-call | flops 399015936 | bytes 9830400 | tf_op jit(solution)/shard_map/pallas_call | solution.py:136
  169.2 5.3 %collective-permute-start.11 = (bf16[6,288,128]{2,1,0:T(8,128)(2,1)S(1)}, bf16[6,288,128]{2,1,0:T(8,128)(2,1)S(1)}, u32[]{:S(2)}, u32[]{:S(2)}) collective-permute-start(bf16[6,288,128]{2,1,0:T(8,128)(2,1)S(1)} %get-tuple-element.17), channel_id=1, source_target_pairs={{1,0},{2,1},{3,2},{4,3},{5,4},{6,5},{7,6},{8,7},{9,8},{10,9},{11,1... | collective-permute-start | bytes 1327112 | tf_op jit(solution)/shard_map/ppermute | solution.py:162
  174.5 19.5 %shard_map.56 = bf16[16,288,128]{2,1,0:T(8,128)(2,1)S(1)} custom-call(bf16[6,288,128]{2,1,0:T(8,128)(2,1)S(1)} %collective-permute-done.6.before, bf16[16,288,128]{2,1,0:T(8,128)(2,1)S(1)} %shard_map.55.owned, bf16[6,288,128]{2,1,0:T(8,128)(2,1)S(1)} %collective-permute-done.7.after, f32[24,10,80,128]{3,2,1,0:T(8,128)S(1)} %pad_maximum_fusion.weights, ...), custom_call_target="tpu_custom_call" | custom-call | flops 399015936 | bytes 9830400 | tf_op jit(solution)/shard_map/pallas_call | solution.py:136
  194.1 19.5 %shard_map.58 = bf16[16,288,128]{2,1,0:T(8,128)(2,1)S(1)} custom-call(bf16[6,288,128]{2,1,0:T(8,128)(2,1)S(1)} %collective-permute-done.10.before, bf16[16,288,128]{2,1,0:T(8,128)(2,1)S(1)} %shard_map.57.owned, bf16[6,288,128]{2,1,0:T(8,128)(2,1)S(1)} %collective-permute-done.11.after, f32[24,10,80,128]{3,2,1,0:T(8,128)S(1)} %pad_maximum_fusion.weights, ...), custom_call_target="tpu_custom_call" | custom-call | flops 399015936 | bytes 9830400 | tf_op jit(solution)/shard_map/pallas_call | solution.py:136
  214.1 2.9 %copy.39 = bf16[8,72,16,128]{3,2,1,0:T(8,128)(2,1)} copy(bf16[8,72,16,128]{3,1,0,2:T(8,128)(2,1)S(1)} %bitcast.53) | data formatting | bytes 4718592 | tf_op jit(solution)/shard_map/transpose | solution.py:199
  (60 shorter events, 11.8 us)
Async XLA Ops:
  0.0 22.2 %copy-start = (bf16[32,64,64]{2,1,0:T(8,128)(2,1)S(1)}, bf16[32,64,64]{2,1,0:T(8,128)(2,1)}, u32[]{:S(2)}) copy-start(bf16[32,64,64]{2,1,0:T(8,128)(2,1)} %param.6) | copy-start | bytes 786436
  0.0 7.3 %copy-start.6 = (bf16[8,72,16,128]{3,2,1,0:T(8,128)(2,1)S(1)}, bf16[8,72,16,128]{3,2,1,0:T(8,128)(2,1)}, u32[]{:S(2)}) copy-start(bf16[8,72,16,128]{3,2,1,0:T(8,128)(2,1)} %param.5) | copy-start | bytes 7077892
  1.8 7.5 %copy-start.2 = (f32[2,72,16,128]{3,1,0,2:T(8,128)}, f32[2,72,16,128]{3,1,0,2:T(8,128)S(1)}, u32[]{:S(2)}) copy-start(f32[2,72,16,128]{3,1,0,2:T(8,128)S(1)} %copy.32) | copy-start | bytes 3538948
  1.9 30.4 %collective-permute-start.2 = (f32[2,72,4,128]{3,1,0,2:T(8,128)S(1)}, f32[2,72,4,128]{3,1,0,2:T(8,128)S(1)}, u32[]{:S(2)}, u32[]{:S(2)}) collective-permute-start(f32[2,72,4,128]{3,1,0,2:T(8,128)S(1)} %get-tuple-element.19), channel_id=1, source_target_pairs={{0,1},{1,2},{2,3},{3,4},{4,5},{5,6},{6,7},{7,8},{8,9},{9,10},{10,1... | collective-permute-start | bytes 884744 | tf_op jit(solution)/shard_map/ppermute | solution.py:161
  2.0 31.1 %collective-permute-start.3 = (f32[2,72,4,128]{3,1,0,2:T(8,128)S(1)}, f32[2,72,4,128]{3,1,0,2:T(8,128)}, u32[]{:S(2)}, u32[]{:S(2)}) collective-permute-start(f32[2,72,4,128]{3,1,0,2:T(8,128)S(1)} %get-tuple-element.20), channel_id=1, source_target_pairs={{1,0},{2,1},{3,2},{4,3},{5,4},{6,5},{7,6},{8,7},{9,8},{10,9},{11,1... | collective-permute-start | bytes 884744 | tf_op jit(solution)/shard_map/ppermute | solution.py:162
  9.3 5.5 %copy-start.7 = (bf16[16,72,72]{2,1,0:T(8,128)(2,1)S(1)}, bf16[16,72,72]{2,1,0:T(8,128)(2,1)}, u32[]{:S(2)}) copy-start(bf16[16,72,72]{2,1,0:T(8,128)(2,1)} %param.9) | copy-start | bytes 497668
  9.3 37.1 %all-to-all-start = ((bf16[8,2,8,72,128]{4,3,2,1,0:T(8,128)(2,1)}), bf16[8,2,8,72,128]{4,3,2,1,0:T(8,128)(2,1)}, u32[]{:S(2)}, u32[]{:S(2)}) async-start(bf16[8,2,8,72,128]{4,3,2,1,0:T(8,128)(2,1)} %bitcast.52), calls=%async_computation | async-start | bytes 4718592 | tf_op jit(solution)/shard_map/all_to_all | solution.py:178
  14.8 16.9 %collective-permute-start.4 = (bf16[4,72,72]{2,1,0:T(8,128)(2,1)S(1)}, bf16[4,72,72]{2,1,0:T(8,128)(2,1)S(1)}, u32[]{:S(2)}, u32[]{:S(2)}) collective-permute-start(bf16[4,72,72]{2,1,0:T(8,128)(2,1)S(1)} %get-tuple-element.22), channel_id=1, source_target_pairs={{0,1},{1,2},{2,3},{3,4},{4,5},{5,6},{6,7},{7,8},{8,9},{9,10},{10,1... | collective-permute-start | bytes 124424 | tf_op jit(solution)/shard_map/ppermute | solution.py:161
  14.9 16.9 %collective-permute-start.5 = (bf16[4,72,72]{2,1,0:T(8,128)(2,1)S(1)}, bf16[4,72,72]{2,1,0:T(8,128)(2,1)S(1)}, u32[]{:S(2)}, u32[]{:S(2)}) collective-permute-start(bf16[4,72,72]{2,1,0:T(8,128)(2,1)S(1)} %get-tuple-element.21), channel_id=1, source_target_pairs={{1,0},{2,1},{3,2},{4,3},{5,4},{6,5},{7,6},{8,7},{9,8},{10,9},{11,1... | collective-permute-start | bytes 124424 | tf_op jit(solution)/shard_map/ppermute | solution.py:162
  31.7 1.3 copy-start.3
  32.3 0.7 copy-start.8
  35.5 0.7 copy-start.4
  65.7 40.0 %all-to-all-start.1 = ((bf16[8,2,8,72,128]{4,3,2,1,0:T(8,128)(2,1)}), bf16[8,2,8,72,128]{4,3,2,1,0:T(8,128)(2,1)}, u32[]{:S(2)}, u32[]{:S(2)}) async-start(bf16[8,2,8,72,128]{4,3,2,1,0:T(8,128)(2,1)} %bitcast.51), calls=%async_computation.1 | async-start | bytes 4718592 | tf_op jit(solution)/shard_map/all_to_all | solution.py:191
  70.3 3.5 %copy-start.5 = (pred[24,1,72,128]{3,2,1,0:T(8,128)(4,1)S(1)}, pred[24,1,72,128]{3,2,1,0:T(8,128)(4,1)}, u32[]{:S(2)}) copy-start(pred[24,1,72,128]{3,2,1,0:T(8,128)(4,1)} %copy-done.4) | copy-start | bytes 663556
  70.3 4.8 %copy-start.9 = (pred[128]{0:T(512)(128)(4,1)S(1)}, pred[128]{0:T(512)(128)(4,1)}, u32[]{:S(2)}) copy-start(pred[128]{0:T(512)(128)(4,1)} %iota_compare_fusion.5) | copy-start | bytes 388
  107.2 17.2 %collective-permute-start = (bf16[6,288,128]{2,1,0:T(8,128)(2,1)S(1)}, bf16[6,288,128]{2,1,0:T(8,128)(2,1)S(1)}, u32[]{:S(2)}, u32[]{:S(2)}) collective-permute-start(bf16[6,288,128]{2,1,0:T(8,128)(2,1)S(1)} %get-tuple-element.11), channel_id=1, source_target_pairs={{0,1},{1,2},{2,3},{3,4},{4,5},{5,6},{6,7},{7,8},{8,9},{9,10},{10,1... | collective-permute-start | bytes 1327112 | tf_op jit(solution)/shard_map/ppermute | solution.py:161
  107.8 16.7 %collective-permute-start.1 = (bf16[6,288,128]{2,1,0:T(8,128)(2,1)S(1)}, bf16[6,288,128]{2,1,0:T(8,128)(2,1)S(1)}, u32[]{:S(2)}, u32[]{:S(2)}) collective-permute-start(bf16[6,288,128]{2,1,0:T(8,128)(2,1)S(1)} %get-tuple-element.9), channel_id=1, source_target_pairs={{1,0},{2,1},{3,2},{4,3},{5,4},{6,5},{7,6},{8,7},{9,8},{10,9},{11,1... | collective-permute-start | bytes 1327112 | tf_op jit(solution)/shard_map/ppermute | solution.py:162
  117.2 32.3 %collective-permute-start.8 = (bf16[6,288,128]{2,1,0:T(8,128)(2,1)S(1)}, bf16[6,288,128]{2,1,0:T(8,128)(2,1)S(1)}, u32[]{:S(2)}, u32[]{:S(2)}) collective-permute-start(bf16[6,288,128]{2,1,0:T(8,128)(2,1)S(1)} %get-tuple-element.10), channel_id=1, source_target_pairs={{0,1},{1,2},{2,3},{3,4},{4,5},{5,6},{6,7},{7,8},{8,9},{9,10},{10,1... | collective-permute-start | bytes 1327112 | tf_op jit(solution)/shard_map/ppermute | solution.py:161
  117.3 32.2 %collective-permute-start.9 = (bf16[6,288,128]{2,1,0:T(8,128)(2,1)S(1)}, bf16[6,288,128]{2,1,0:T(8,128)(2,1)S(1)}, u32[]{:S(2)}, u32[]{:S(2)}) collective-permute-start(bf16[6,288,128]{2,1,0:T(8,128)(2,1)S(1)} %get-tuple-element.12), channel_id=1, source_target_pairs={{1,0},{2,1},{3,2},{4,3},{5,4},{6,5},{7,6},{8,7},{9,8},{10,9},{11,1... | collective-permute-start | bytes 1327112 | tf_op jit(solution)/shard_map/ppermute | solution.py:162
  144.1 30.5 %collective-permute-start.6 = (bf16[6,288,128]{2,1,0:T(8,128)(2,1)S(1)}, bf16[6,288,128]{2,1,0:T(8,128)(2,1)S(1)}, u32[]{:S(2)}, u32[]{:S(2)}) collective-permute-start(bf16[6,288,128]{2,1,0:T(8,128)(2,1)S(1)} %get-tuple-element.16), channel_id=1, source_target_pairs={{0,1},{1,2},{2,3},{3,4},{4,5},{5,6},{6,7},{7,8},{8,9},{9,10},{10,1... | collective-permute-start | bytes 1327112 | tf_op jit(solution)/shard_map/ppermute | solution.py:161
  144.1 30.4 %collective-permute-start.7 = (bf16[6,288,128]{2,1,0:T(8,128)(2,1)S(1)}, bf16[6,288,128]{2,1,0:T(8,128)(2,1)S(1)}, u32[]{:S(2)}, u32[]{:S(2)}) collective-permute-start(bf16[6,288,128]{2,1,0:T(8,128)(2,1)S(1)} %get-tuple-element.15), channel_id=1, source_target_pairs={{1,0},{2,1},{3,2},{4,3},{5,4},{6,5},{7,6},{8,7},{9,8},{10,9},{11,1... | collective-permute-start | bytes 1327112 | tf_op jit(solution)/shard_map/ppermute | solution.py:162
  169.1 25.0 %collective-permute-start.10 = (bf16[6,288,128]{2,1,0:T(8,128)(2,1)S(1)}, bf16[6,288,128]{2,1,0:T(8,128)(2,1)S(1)}, u32[]{:S(2)}, u32[]{:S(2)}) collective-permute-start(bf16[6,288,128]{2,1,0:T(8,128)(2,1)S(1)} %get-tuple-element.18), channel_id=1, source_target_pairs={{0,1},{1,2},{2,3},{3,4},{4,5},{5,6},{6,7},{7,8},{8,9},{9,10},{10,1... | collective-permute-start | bytes 1327112 | tf_op jit(solution)/shard_map/ppermute | solution.py:161
  169.2 24.9 %collective-permute-start.11 = (bf16[6,288,128]{2,1,0:T(8,128)(2,1)S(1)}, bf16[6,288,128]{2,1,0:T(8,128)(2,1)S(1)}, u32[]{:S(2)}, u32[]{:S(2)}) collective-permute-start(bf16[6,288,128]{2,1,0:T(8,128)(2,1)S(1)} %get-tuple-element.17), channel_id=1, source_target_pairs={{1,0},{2,1},{3,2},{4,3},{5,4},{6,5},{7,6},{8,7},{9,8},{10,9},{11,1... | collective-permute-start | bytes 1327112 | tf_op jit(solution)/shard_map/ppermute | solution.py:162
  213.9 3.2 %copy-start.1 = (bf16[32,64,64]{2,1,0:T(8,128)(2,1)S(1)}, bf16[32,64,64]{2,1,0:T(8,128)(2,1)}, u32[]{:S(2)}) copy-start(bf16[32,64,64]{2,1,0:T(8,128)(2,1)} %param.6) | copy-start | bytes 786436
where the time goes:
time: 218 us; the launch traced here: 217 us
  Pallas kernels  78.1 us (36%)
  starting transfers between devices  42.6 us (20%)
  local copies, waits for them, and re-layouts  35.2 us (16%)
  waiting for transfers between devices  31.6 us (14%)
  other arithmetic  22.5 us (10%)
  matrix products  6.76 us (3%)
    pallas_call x4, Pallas kernels, advect(): pl.pallas_call(functools.partial(advect_kernel, steps, rows), out_shape=j...  78.1 us
    ppermute x6, starting transfers between devices, from_sides(): lax.ppermute(lax.slice_in_dim(array, 0, width, axis=dim), 'tile', down)  31.6 us
    all_to_all x1, waiting for transfers between devices, shards(): lax.all_to_all(blended, 'mem', split_axis=0, concat_axis=0, tiled=True)  22.7 us
    unnamed x9, other arithmetic  12.8 us
    gather x2, local copies, waits for them, and re-layouts, shards(): chosen = jnp.take(weights, patches, axis=0)  9.48 us
    all_to_all x1, waiting for transfers between devices, shards(): lax.all_to_all(to_send, 'mem', split_axis=0, concat_axis=0, tiled=True)  8.85 us
    dot_general x1, matrix products, shards(): jnp.einsum('ijco,iclj->iolj', chosen, jnp.transpose(arrived, (1, 0, 2, 3,...  6.76 us
    reshape x1, local copies, waits for them, and re-layouts, shards(): blended.reshape(share, peers, members, levels, lanes)  6.26 us
  transfers between devices with their start and end apart: 14, of which 2 were waited for; matrix products, arithmetic and copies ran while one was open for 17% of the time, Pallas kernels for 27%

commit v1 on v0

v1 whole, which is shorter than its diff:
```python
import functools

import jax
import jax.numpy as jnp
from jax import lax
from jax.experimental import pallas as pl
from jax.experimental.pallas import tpu as pltpu
from jax.sharding import PartitionSpec as P

HALF = 3
GROUPS = 2
LEVELS = 72
PAIR = 2 * LEVELS
TILE_ROWS = 16
LANES = 128


def stencil_weights(numbers):
    location = -jnp.abs(numbers)
    below, above, further = location - 1.0, location + 1.0, location + 2.0
    inner, outer = location * below, further * above
    far = above * inner * (-1.0 / 6.0)
    near = further * inner * 0.5
    mid = outer * below * -0.5
    ahead = outer * location * (1.0 / 6.0)
    forward = numbers >= 0.0
    return [
        jnp.where(forward, far, 0.0),
        jnp.where(forward, near, ahead),
        mid,
        jnp.where(forward, ahead, near),
        jnp.where(forward, 0.0, far),
    ]


def weighted(values, weights):
    total = values[0] * weights[0]
    for value, weight in zip(values[1:], weights[1:]):
        total = total + value * weight
    return total


def advect_kernel(steps, first, low, high, numbers, inverse, out, staged, field, other, across_0, across_1,
                  number, weight, operator, field_sem, number_sem, operator_sem):
    length, rows, _ = out.shape
    computed = length + 4 * (steps - 1)
    pairs = rows // PAIR
    loads = [
        pltpu.make_async_copy(low, staged.at[pl.ds(0, low.shape[0])], field_sem.at[0]),
        pltpu.make_async_copy(high, staged.at[pl.ds(low.shape[0], high.shape[0])], field_sem.at[1]),
        pltpu.make_async_copy(numbers.at[pl.ds(first, computed)], number, number_sem),
        pltpu.make_async_copy(inverse.at[pl.ds(first, computed)], operator, operator_sem),
    ]
    for load in loads:
        load.start()
    for load in loads:
        load.wait()

    lane = lax.broadcasted_iota(jnp.int32, (8, LANES), 1)
    last = LANES - 1
    inside = [lane >= 2, lane >= 1, None, lane <= last - 1, lane <= last - 2]

    def prepare(column):
        for level in range(0, LEVELS, 8):
            at = pl.ds(level, 8)
            lon = stencil_weights(number[column, 0, at, :])
            lat = stencil_weights(number[column, 1, at, :])
            lat = [w if keep is None else jnp.where(keep, w, 0.0) for keep, w in zip(inside, lat)]
            for k, w in enumerate(lon + lat):
                weight[column, k, at, :] = w
                if level == 0:
                    weight[column, k, pl.ds(LEVELS, 8), :] = w

    def widen(column):
        field[column] = staged[column].astype(jnp.float32)

    def stencils(source, column, w_column, across):
        def lat_part(at, along, w):
            near = along.astype(jnp.bfloat16)
            shifted = [pltpu.roll(near, turn, 1).astype(jnp.float32) if turn else along
                       for turn in (2, 1, 0, LANES - 1, LANES - 2)]
            across[at, :] = weighted(shifted, w).astype(jnp.bfloat16)

        for tile in range(PAIR // TILE_ROWS):
            level = (tile * TILE_ROWS) % LEVELS
            w = [weight[w_column, k, pl.ds(level, TILE_ROWS), :] for k in range(10)]
            for pair in range(pairs):
                at = pl.ds(pair * PAIR + tile * TILE_ROWS, TILE_ROWS)
                lat_part(at, weighted([source[column + k, at, :] for k in range(5)], w[:5]), w[5:])

    def vertical(across, target, column, w_column):
        side = jnp.concatenate([across[pl.ds(pair * PAIR, PAIR), :] for pair in range(pairs)], axis=1)
        mixed = jnp.dot(operator[w_column], side, preferred_element_type=jnp.float32).astype(jnp.bfloat16)
        for pair in range(pairs):
            target[column, pl.ds(pair * PAIR, PAIR), :] = mixed[:, pair * LANES:(pair + 1) * LANES].astype(target.dtype)

    buffers = (field, other)
    for step in range(steps):
        source = buffers[step % 2]
        target = out if step == steps - 1 else buffers[(step + 1) % 2]
        columns = length + 4 * (steps - 1 - step)
        shift = 2 * step

        def ready(column):
            if step == 0:
                widen(column + 4)
                prepare(column)

        if step == 0:
            for column in range(4):
                widen(column)
        ready(0)
        ready(1)
        stencils(source, 0, shift, across_0)
        stencils(source, 1, shift + 1, across_1)

        def two_columns(index, carry):
            even = 2 * index
            vertical(across_0, target, even - 2, shift + even - 2)
            vertical(across_1, target, even - 1, shift + even - 1)
            ready(even)
            ready(even + 1)
            stencils(source, even, shift + even, across_0)
            stencils(source, even + 1, shift + even + 1, across_1)
            return carry

        lax.fori_loop(1, columns // 2, two_columns, 0)
        vertical(across_0, target, columns - 2, shift + columns - 2)
        vertical(across_1, target, columns - 1, shift + columns - 1)


def advect(steps, first, low, high, numbers, inverse):
    rows, lanes = low.shape[1:]
    wide = low.shape[0] + high.shape[0]
    length, computed = wide - 4 * steps, wide - 4
    anywhere = pl.BlockSpec(memory_space=pl.ANY)
    work = (length + 2 * steps) * steps * rows * lanes
    return pl.pallas_call(
        functools.partial(advect_kernel, steps, first),
        out_shape=jax.ShapeDtypeStruct((length, rows, lanes), low.dtype),
        in_specs=[anywhere] * 4,
        out_specs=pl.BlockSpec(memory_space=pltpu.VMEM),
        scratch_shapes=[
            pltpu.VMEM((wide, rows, lanes), jnp.bfloat16),
            pltpu.VMEM((wide, rows, lanes), jnp.float32),
            pltpu.VMEM((wide, rows, lanes), jnp.float32),
            pltpu.VMEM((rows, lanes), jnp.bfloat16),
            pltpu.VMEM((rows, lanes), jnp.bfloat16),
            pltpu.VMEM((computed,) + numbers.shape[1:], jnp.float32),
            pltpu.VMEM((computed, 10, LEVELS + 8, lanes), jnp.float32),
            pltpu.VMEM((computed,) + inverse.shape[1:], jnp.bfloat16),
            pltpu.SemaphoreType.DMA((2,)),
            pltpu.SemaphoreType.DMA,
            pltpu.SemaphoreType.DMA,
        ],
        compiler_params=pltpu.CompilerParams(vmem_limit_bytes=36 * 1024 * 1024),
        cost_estimate=pl.CostEstimate(flops=work * (2 * LEVELS + 20), bytes_accessed=numbers.size * 4, transcendentals=0),
    )(low, high, numbers, inverse)


def from_below(array, width):
    peers = lax.axis_size("tile")
    return lax.ppermute(array[array.shape[0] - width:], "tile", [(i, (i + 1) % peers) for i in range(peers)])


def from_above(array, width):
    peers = lax.axis_size("tile")
    return lax.ppermute(array[:width], "tile", [((i + 1) % peers, i) for i in range(peers)])


def shards(ensemble, weights, patch_index, courant, vert_inverse):
    peers = lax.axis_size("mem")
    members, levels, length, lanes = ensemble.shape
    share = length // peers
    halo, shift = 4 * HALF, 2 * HALF
    below, above = shift - 2, halo - 2

    to_send = jnp.transpose(ensemble.reshape(members, levels, peers, share, lanes), (3, 2, 0, 1, 4))
    patches = lax.dynamic_slice_in_dim(patch_index, lax.axis_index("mem") * share, share, 0)
    chosen = jnp.take(weights, patches, axis=0)

    arrived = [lax.all_to_all(to_send[part], "mem", split_axis=0, concat_axis=0, tiled=True) for part in range(share)]
    tied, _ = lax.optimization_barrier(((courant, vert_inverse), to_send))
    numbers, inverse = jnp.transpose(tied[0], (2, 0, 1, 3)), tied[1]
    numbers = jnp.concatenate([from_below(numbers, below), numbers, from_above(numbers, above)])
    inverse = jnp.concatenate([from_below(inverse, below), inverse, from_above(inverse, above)])
    empty = jnp.zeros_like(inverse)
    inverse = jnp.concatenate([jnp.concatenate([inverse, empty], 2), jnp.concatenate([empty, inverse], 2)], 1)

    returned = []
    for part in range(share):
        blended = jnp.einsum("jco,clj->olj", chosen[part], arrived[part].reshape(-1, levels, lanes),
                             preferred_element_type=jnp.float32).astype(jnp.bfloat16)
        blended = blended.reshape(arrived[part].shape)
        returned.append(lax.all_to_all(blended, "mem", split_axis=0, concat_axis=0, tiled=True))
    analysed = jnp.stack(returned, axis=1).reshape(length, GROUPS, -1, lanes)
    fields = [analysed[:, group] for group in range(GROUPS)]
    fields = [advect(HALF, below + 2, field, from_above(field, halo), numbers, inverse) for field in fields]
    fields = [advect(HALF, 0, from_below(field, halo), field, numbers, inverse) for field in fields]
    forecast = jnp.stack(fields, axis=1).reshape(length, members, levels, lanes)
    return jnp.transpose(forecast, (1, 2, 0, 3))


def solution(mesh):
    return jax.shard_map(
        shards,
        mesh=mesh,
        in_specs=(
            P("mem", None, "tile", None),
            P("tile", None, None),
            P("tile", None),
            P(None, None, "tile", None),
            P("tile", None, None),
        ),
        out_specs=P("mem", None, "tile", None),
        check_vma=False,
    )
```

time: 218 us -> 192 us (0.88)
  the two profiles are of different devices: /device:TPU:128 before, /device:TPU:193 now
where the time goes in v1:
time: 192 us; the launch traced here: 191 us
  starting transfers between devices  55 us (29%)
  Pallas kernels  43.4 us (23%)
  waiting for transfers between devices  40.1 us (21%)
  local copies, waits for them, and re-layouts  36 us (19%)
  other arithmetic  8.87 us (5%)
  matrix products  7.21 us (4%)
    pallas_call x4, Pallas kernels, advect(): pl.pallas_call(functools.partial(advect_kernel, steps, first), out_shape=...  43.4 us
    ppermute x4, starting transfers between devices, from_below(): lax.ppermute(array[array.shape[0] - width:], 'tile', [(i, (i + 1) % peers...  31.9 us
    all_to_all x2, waiting for transfers between devices, shards(): lax.all_to_all(to_send[part], 'mem', split_axis=0, concat_axis=0, tiled=T...  16.1 us
    ppermute x4, waiting for transfers between devices, from_below(): lax.ppermute(array[array.shape[0] - width:], 'tile', [(i, (i + 1) % peers...  11.3 us
    gather x2, local copies, waits for them, and re-layouts, shards(): chosen = jnp.take(weights, patches, axis=0)  9.46 us
    all_to_all x2, starting transfers between devices, shards(): lax.all_to_all(to_send[part], 'mem', split_axis=0, concat_axis=0, tiled=T...  9.28 us
    all_to_all x2, starting transfers between devices, shards(): lax.all_to_all(blended, 'mem', split_axis=0, concat_axis=0, tiled=True)  8.78 us
    reshape x2, local copies, waits for them, and re-layouts, shards(): blended = blended.reshape(arrived[part].shape)  7.82 us
  transfers between devices with their start and end apart: 12, of which 4 were waited for; matrix products, arithmetic and copies ran while one was open for 24% of the time, Pallas kernels for 17%

profile of v1, /device:TPU:193, one launch (start us, length us, event | category | flops | bytes accessed | tf_op | source)
XLA Modules:
  0.0 190.8 jit_solution(9643560709046164226)
XLA Ops:
  0.0 2.3 %copy.33 = bf16[8,72,16,128]{3,1,2,0:T(8,128)(2,1)S(1)} copy(bf16[8,72,16,128]{3,2,1,0:T(8,128)(2,1)} %param.5) | data formatting | bytes 4718592 | tf_op args[0]
  2.5 1.2 copy.34
  3.7 5.0 %all-to-all-start = ((bf16[8,8,72,128]{3,2,1,0:T(8,128)(2,1)}), bf16[8,8,72,128]{3,2,1,0:T(8,128)(2,1)S(1)}, u32[]{:S(2)}, u32[]{:S(2)}) async-start(bf16[8,8,72,128]{3,2,1,0:T(8,128)(2,1)} %copy.34), calls=%async_computation | async-start | bytes 2359296 | tf_op jit(solution)/shard_map/all_to_all | solution.py:182
  8.7 1.2 copy.37
  9.9 16.1 %all-to-all-done = bf16[8,8,72,128]{3,2,1,0:T(8,128)(2,1)S(1)} async-done(((bf16[8,8,72,128]{3,2,1,0:T(8,128)(2,1)}), bf16[8,8,72,128]{3,2,1,0:T(8,128)(2,1)S(1)}, u32[]{:S(2)}, u32[]{:S(2)}) %all-to-all-start) | async-done | bytes 1179680 | tf_op jit(solution)/shard_map/all_to_all | solution.py:182
  26.0 4.2 %all-to-all-start.2 = ((bf16[8,8,72,128]{3,2,1,0:T(8,128)(2,1)}), bf16[8,8,72,128]{3,2,1,0:T(8,128)(2,1)}, u32[]{:S(2)}, u32[]{:S(2)}) async-start(bf16[8,8,72,128]{3,2,1,0:T(8,128)(2,1)} %copy.37), calls=%async_computation.2 | async-start | bytes 2359296 | tf_op jit(solution)/shard_map/all_to_all | solution.py:182
  30.9 3.0 %gather_fusion = bf16[256,64,64]{2,1,0:T(8,128)(2,1)} fusion(bf16[32,64,64]{2,1,0:T(8,128)(2,1)S(1)} %copy-done, s32[1024]{0:T(1024)S(1)} %pad_clamp_fusion), kind=kCustom, calls=%fused_computation | custom fusion | bytes 4195328 | tf_op jit(solution)/shard_map/jit(_take)/gather | solution.py:180
  34.0 6.4 %copy.32 = bf16[256,64,64]{1,2,0:T(8,128)(2,1)} copy(bf16[256,64,64]{2,1,0:T(8,128)(2,1)} %gather_fusion) | data formatting | bytes 4194304 | tf_op jit(solution)/shard_map/jit(_take)/gather | solution.py:180
  41.1 3.8 %broadcast_select_fusion = bf16[2,128,64,64]{2,3,1,0:T(8,128)(2,1)} fusion(bf16[2,128,64,64]{2,3,1,0:T(8,128)(2,1)} %bitcast.69, pred[2,128]{1,0:T(4,128)(4,1)S(1)} %compare_and_fusion), kind=kLoop, calls=%fused_computation.5 | loop fusion | flops 1048576 | bytes 4194560 | tf_op jit(solution)/shard_map/jit(_take)/select_n | solution.py:180
  44.9 3.1 %copy.35 = bf16[8,8,72,128]{2,1,0,3:T(8,128)(2,1)S(1)} copy(bf16[8,8,72,128]{3,2,1,0:T(8,128)(2,1)} %copy-done.2) | data formatting | bytes 2359296 | tf_op jit(solution)/shard_map/all_to_all | solution.py:182
  48.0 3.6 %convert_bitcast_fusion.1 = bf16[8,8,72,128]{2,1,0,3:T(8,128)(2,1)} fusion(bf16[8,8,72,128]{2,1,0,3:T(8,128)(2,1)S(1)} %copy.35, bf16[2,128,64,64]{2,3,1,0:T(8,128)(2,1)} %broadcast_select_fusion), kind=kOutput, calls=%fused_computation.17 | convolution fusion | flops 76087296 | bytes 4456448 | tf_op jit(solution)/shard_map/jco,clj->olj/dot_general | solution.py:192
  51.6 3.9 %copy.36 = bf16[8,8,72,128]{3,2,1,0:T(8,128)(2,1)} copy(bf16[8,8,72,128]{2,1,0,3:T(8,128)(2,1)} %convert_bitcast_fusion.1) | data formatting | bytes 2359296 | tf_op jit(solution)/shard_map/reshape | solution.py:194
  55.5 5.0 %all-to-all-start.1 = ((bf16[8,8,72,128]{3,2,1,0:T(8,128)(2,1)}), bf16[8,8,72,128]{3,2,1,0:T(8,128)(2,1)}, u32[]{:S(2)}, u32[]{:S(2)}) async-start(bf16[8,8,72,128]{3,2,1,0:T(8,128)(2,1)} %copy.36), calls=%async_computation.1 | async-start | bytes 2359296 | tf_op jit(solution)/shard_map/all_to_all | solution.py:195
  60.5 3.1 %copy.38 = bf16[8,8,72,128]{2,1,0,3:T(8,128)(2,1)S(1)} copy(bf16[8,8,72,128]{3,2,1,0:T(8,128)(2,1)} %all-to-all-done.2) | data formatting | bytes 2359296 | tf_op jit(solution)/shard_map/all_to_all | solution.py:182
  63.6 3.6 %convert_bitcast_fusion = bf16[8,8,72,128]{2,1,0,3:T(8,128)(2,1)} fusion(bf16[8,8,72,128]{2,1,0,3:T(8,128)(2,1)S(1)} %copy.38, bf16[2,128,64,64]{2,3,1,0:T(8,128)(2,1)} %broadcast_select_fusion), kind=kOutput, calls=%fused_computation.16 | convolution fusion | flops 76087296 | bytes 4456448 | tf_op jit(solution)/shard_map/jco,clj->olj/dot_general | solution.py:192
  67.2 3.9 %copy.39 = bf16[8,8,72,128]{3,2,1,0:T(8,128)(2,1)} copy(bf16[8,8,72,128]{2,1,0,3:T(8,128)(2,1)} %convert_bitcast_fusion) | data formatting | bytes 2359296 | tf_op jit(solution)/shard_map/reshape | solution.py:194
  71.2 5.1 %all-to-all-done.1 = bf16[8,8,72,128]{3,2,1,0:T(8,128)(2,1)} async-done(((bf16[8,8,72,128]{3,2,1,0:T(8,128)(2,1)}), bf16[8,8,72,128]{3,2,1,0:T(8,128)(2,1)}, u32[]{:S(2)}, u32[]{:S(2)}) %all-to-all-start.1) | async-done | bytes 1179680 | tf_op jit(solution)/shard_map/all_to_all | solution.py:195
  76.3 3.7 %all-to-all-start.3 = ((bf16[8,8,72,128]{3,2,1,0:T(8,128)(2,1)}), bf16[8,8,72,128]{3,2,1,0:T(8,128)(2,1)S(1)}, u32[]{:S(2)}, u32[]{:S(2)}) async-start(bf16[8,8,72,128]{3,2,1,0:T(8,128)(2,1)} %copy.39), calls=%async_computation.3 | async-start | bytes 2359296 | tf_op jit(solution)/shard_map/all_to_all | solution.py:195
  80.1 4.9 %collective-permute-start.3 = (bf16[4,72,72]{2,1,0:T(8,128)(2,1)S(1)}, bf16[4,72,72]{2,1,0:T(8,128)(2,1)S(1)}, u32[]{:S(2)}, u32[]{:S(2)}) collective-permute-start(bf16[4,72,72]{2,1,0:T(8,128)(2,1)S(1)} %slice.59), channel_id=1, source_target_pairs={{0,1},{1,2},{2,3},{3,4},{4,5},{5,6},{6,7},{7,8},{8,9},{9,10},{10,1... | collective-permute-start | bytes 124424 | tf_op jit(solution)/shard_map/ppermute | solution.py:163
  84.9 1.7 copy.52
  88.2 3.2 %collective-permute-start.1 = (f32[4,2,72,128]{3,2,1,0:T(8,128)}, f32[4,2,72,128]{3,2,1,0:T(8,128)}, u32[]{:S(2)}, u32[]{:S(2)}) collective-permute-start(f32[4,2,72,128]{3,2,1,0:T(8,128)} %slice.74), channel_id=1, source_target_pairs={{0,1},{1,2},{2,3},{3,4},{4,5},{5,6},{6,7},{7,8},{8,9},{9,10},{10,1... | collective-permute-start | bytes 884744 | tf_op jit(solution)/shard_map/ppermute | solution.py:163
  92.2 11.3 %collective-permute-done.3 = bf16[4,72,72]{2,1,0:T(8,128)(2,1)S(1)} collective-permute-done((bf16[4,72,72]{2,1,0:T(8,128)(2,1)S(1)}, bf16[4,72,72]{2,1,0:T(8,128)(2,1)S(1)}, u32[]{:S(2)}, u32[]{:S(2)}) %collective-permute-start.3) | collective-permute-done | bytes 41504 | tf_op jit(solution)/shard_map/ppermute | solution.py:163
  103.5 1.5 pad_maximum_fusion
  105.2 4.8 %collective-permute-start = (bf16[12,288,128]{2,1,0:T(8,128)(2,1)S(1)}, bf16[12,288,128]{2,1,0:T(8,128)(2,1)S(1)}, u32[]{:S(2)}, u32[]{:S(2)}) collective-permute-start(bf16[12,288,128]{2,1,0:T(8,128)(2,1)S(1)} %get-tuple-element.9), channel_id=1, source_target_pairs={{1,0},{2,1},{3,2},{4,3},{5,4},{6,5},{7,6},{8,7},{9,8},{10,9},{11,1... | collective-permute-start | bytes 2654216 | tf_op jit(solution)/shard_map/ppermute | solution.py:168
  111.0 1.3 pad_maximum_fusion.2.numbers
  112.5 7.5 %collective-permute-done.high = bf16[12,288,128]{2,1,0:T(8,128)(2,1)S(1)} collective-permute-done((bf16[12,288,128]{2,1,0:T(8,128)(2,1)S(1)}, bf16[12,288,128]{2,1,0:T(8,128)(2,1)S(1)}, u32[]{:S(2)}, u32[]{:S(2)}) %collective-permute-start) | collective-permute-done | bytes 884768 | tf_op jit(solution)/shard_map/ppermute | solution.py:168
  120.0 10.9 %shard_map.55.high = bf16[16,288,128]{2,1,0:T(8,128)(2,1)S(1)} custom-call(bf16[16,288,128]{2,1,0:T(8,128)(2,1)S(1)} %get-tuple-element.11.low, bf16[12,288,128]{2,1,0:T(8,128)(2,1)S(1)} %collective-permute-done.high, f32[30,2,72,128]{3,2,1,0:T(8,128)S(1)} %pad_maximum_fusion.2.numbers, bf16[30,144,144]{2,1,0:T(8,128)(2,1)S(1)} %fusion.2.inverse), custom_call_target="tpu_custom_call" | custom-call | flops 399015936 | bytes 2211840 | tf_op jit(solution)/shard_map/pallas_call | solution.py:138
  131.0 10.9 %shard_map.57.high = bf16[16,288,128]{2,1,0:T(8,128)(2,1)S(1)} custom-call(bf16[16,288,128]{2,1,0:T(8,128)(2,1)S(1)} %get-tuple-element.12.low, bf16[12,288,128]{2,1,0:T(8,128)(2,1)S(1)} %collective-permute-done.6.high, f32[30,2,72,128]{3,2,1,0:T(8,128)S(1)} %pad_maximum_fusion.2.numbers, bf16[30,144,144]{2,1,0:T(8,128)(2,1)S(1)} %fusion.2.inverse), custom_call_target="tpu_custom_call" | custom-call | flops 399015936 | bytes 2211840 | tf_op jit(solution)/shard_map/pallas_call | solution.py:138
  141.9 23.7 %collective-permute-start.7 = (bf16[12,288,128]{2,1,0:T(8,128)(2,1)S(1)}, bf16[12,288,128]{2,1,0:T(8,128)(2,1)S(1)}, u32[]{:S(2)}, u32[]{:S(2)}) collective-permute-start(bf16[12,288,128]{2,1,0:T(8,128)(2,1)S(1)} %slice.79), channel_id=1, source_target_pairs={{0,1},{1,2},{2,3},{3,4},{4,5},{5,6},{6,7},{7,8},{8,9},{9,10},{10,1... | collective-permute-start | bytes 2654216 | tf_op jit(solution)/shard_map/ppermute | solution.py:163
  165.7 10.9 %shard_map.56 = bf16[16,288,128]{2,1,0:T(8,128)(2,1)S(1)} custom-call(bf16[12,288,128]{2,1,0:T(8,128)(2,1)S(1)} %collective-permute-done.5.low, bf16[16,288,128]{2,1,0:T(8,128)(2,1)S(1)} %shard_map.55.high, f32[30,2,72,128]{3,2,1,0:T(8,128)S(1)} %pad_maximum_fusion.2.numbers, bf16[30,144,144]{2,1,0:T(8,128)(2,1)S(1)} %fusion.2.inverse), custom_call_target="tpu_custom_call" | custom-call | flops 399015936 | bytes 2211840 | tf_op jit(solution)/shard_map/pallas_call | solution.py:138
  176.5 10.9 %shard_map.58 = bf16[16,288,128]{2,1,0:T(8,128)(2,1)S(1)} custom-call(bf16[12,288,128]{2,1,0:T(8,128)(2,1)S(1)} %collective-permute-done.7.low, bf16[16,288,128]{2,1,0:T(8,128)(2,1)S(1)} %shard_map.57.high, f32[30,2,72,128]{3,2,1,0:T(8,128)S(1)} %pad_maximum_fusion.2.numbers, bf16[30,144,144]{2,1,0:T(8,128)(2,1)S(1)} %fusion.2.inverse), custom_call_target="tpu_custom_call" | custom-call | flops 399015936 | bytes 2211840 | tf_op jit(solution)/shard_map/pallas_call | solution.py:138
  187.9 2.9 %copy.46 = bf16[8,72,16,128]{3,2,1,0:T(8,128)(2,1)} copy(bf16[8,72,16,128]{3,1,0,2:T(8,128)(2,1)S(1)} %bitcast.74) | data formatting | bytes 4718592 | tf_op jit(solution)/shard_map/transpose | solution.py:201
  (38 shorter events, 5.9 us)
Async XLA Ops:
  0.0 30.9 %copy-start = (bf16[32,64,64]{2,1,0:T(8,128)(2,1)S(1)}, bf16[32,64,64]{2,1,0:T(8,128)(2,1)}, u32[]{:S(2)}) copy-start(bf16[32,64,64]{2,1,0:T(8,128)(2,1)} %param.6) | copy-start | bytes 786436
  3.7 22.3 %all-to-all-start = ((bf16[8,8,72,128]{3,2,1,0:T(8,128)(2,1)}), bf16[8,8,72,128]{3,2,1,0:T(8,128)(2,1)S(1)}, u32[]{:S(2)}, u32[]{:S(2)}) async-start(bf16[8,8,72,128]{3,2,1,0:T(8,128)(2,1)} %copy.34), calls=%async_computation | async-start | bytes 2359296 | tf_op jit(solution)/shard_map/all_to_all | solution.py:182
  26.0 8.0 %copy-start.2 = (bf16[8,8,72,128]{3,2,1,0:T(8,128)(2,1)}, bf16[8,8,72,128]{3,2,1,0:T(8,128)(2,1)S(1)}, u32[]{:S(2)}) copy-start(bf16[8,8,72,128]{3,2,1,0:T(8,128)(2,1)S(1)} %all-to-all-done) | copy-start | bytes 3538948
  26.0 29.5 %all-to-all-start.2 = ((bf16[8,8,72,128]{3,2,1,0:T(8,128)(2,1)}), bf16[8,8,72,128]{3,2,1,0:T(8,128)(2,1)}, u32[]{:S(2)}, u32[]{:S(2)}) async-start(bf16[8,8,72,128]{3,2,1,0:T(8,128)(2,1)} %copy.37), calls=%async_computation.2 | async-start | bytes 2359296 | tf_op jit(solution)/shard_map/all_to_all | solution.py:182
  55.5 20.8 %all-to-all-start.1 = ((bf16[8,8,72,128]{3,2,1,0:T(8,128)(2,1)}), bf16[8,8,72,128]{3,2,1,0:T(8,128)(2,1)}, u32[]{:S(2)}, u32[]{:S(2)}) async-start(bf16[8,8,72,128]{3,2,1,0:T(8,128)(2,1)} %copy.36), calls=%async_computation.1 | async-start | bytes 2359296 | tf_op jit(solution)/shard_map/all_to_all | solution.py:195
  67.2 12.8 %copy-start.3 = (bf16[16,72,72]{2,1,0:T(8,128)(2,1)S(1)}, bf16[16,72,72]{2,1,0:T(8,128)(2,1)}, u32[]{:S(2)}) copy-start(bf16[16,72,72]{2,1,0:T(8,128)(2,1)} %param.9) | copy-start | bytes 497668
  76.3 27.2 %all-to-all-start.3 = ((bf16[8,8,72,128]{3,2,1,0:T(8,128)(2,1)}), bf16[8,8,72,128]{3,2,1,0:T(8,128)(2,1)S(1)}, u32[]{:S(2)}, u32[]{:S(2)}) async-start(bf16[8,8,72,128]{3,2,1,0:T(8,128)(2,1)} %copy.39), calls=%async_computation.3 | async-start | bytes 2359296 | tf_op jit(solution)/shard_map/all_to_all | solution.py:195
  80.1 23.4 %collective-permute-start.3 = (bf16[4,72,72]{2,1,0:T(8,128)(2,1)S(1)}, bf16[4,72,72]{2,1,0:T(8,128)(2,1)S(1)}, u32[]{:S(2)}, u32[]{:S(2)}) collective-permute-start(bf16[4,72,72]{2,1,0:T(8,128)(2,1)S(1)} %slice.59), channel_id=1, source_target_pairs={{0,1},{1,2},{2,3},{3,4},{4,5},{5,6},{6,7},{7,8},{8,9},{9,10},{10,1... | collective-permute-start | bytes 124424 | tf_op jit(solution)/shard_map/ppermute | solution.py:163
  87.5 23.5 %collective-permute-start.2 = (f32[10,2,72,128]{3,2,1,0:T(8,128)}, f32[10,2,72,128]{3,2,1,0:T(8,128)}, u32[]{:S(2)}, u32[]{:S(2)}) collective-permute-start(f32[10,2,72,128]{3,2,1,0:T(8,128)} %slice.75), channel_id=1, source_target_pairs={{1,0},{2,1},{3,2},{4,3},{5,4},{6,5},{7,6},{8,7},{9,8},{10,9},{11,1... | collective-permute-start | bytes 2211848 | tf_op jit(solution)/shard_map/ppermute | solution.py:168
  88.2 22.7 %collective-permute-start.1 = (f32[4,2,72,128]{3,2,1,0:T(8,128)}, f32[4,2,72,128]{3,2,1,0:T(8,128)}, u32[]{:S(2)}, u32[]{:S(2)}) collective-permute-start(f32[4,2,72,128]{3,2,1,0:T(8,128)} %slice.74), channel_id=1, source_target_pairs={{0,1},{1,2},{2,3},{3,4},{4,5},{5,6},{6,7},{7,8},{8,9},{9,10},{10,1... | collective-permute-start | bytes 884744 | tf_op jit(solution)/shard_map/ppermute | solution.py:163
  92.2 18.1 %collective-permute-start.4 = (bf16[10,72,72]{2,1,0:T(8,128)(2,1)}, bf16[10,72,72]{2,1,0:T(8,128)(2,1)S(1)}, u32[]{:S(2)}, u32[]{:S(2)}) collective-permute-start(bf16[10,72,72]{2,1,0:T(8,128)(2,1)} %slice.60), channel_id=1, source_target_pairs={{1,0},{2,1},{3,2},{4,3},{5,4},{6,5},{7,6},{8,7},{9,8},{10,9},{11,1... | collective-permute-start | bytes 311048 | tf_op jit(solution)/shard_map/ppermute | solution.py:168
  105.2 14.8 %collective-permute-start = (bf16[12,288,128]{2,1,0:T(8,128)(2,1)S(1)}, bf16[12,288,128]{2,1,0:T(8,128)(2,1)S(1)}, u32[]{:S(2)}, u32[]{:S(2)}) collective-permute-start(bf16[12,288,128]{2,1,0:T(8,128)(2,1)S(1)} %get-tuple-element.9), channel_id=1, source_target_pairs={{1,0},{2,1},{3,2},{4,3},{5,4},{6,5},{7,6},{8,7},{9,8},{10,9},{11,1... | collective-permute-start | bytes 2654216 | tf_op jit(solution)/shard_map/ppermute | solution.py:168
  110.0 21.0 %collective-permute-start.6 = (bf16[12,288,128]{2,1,0:T(8,128)(2,1)S(1)}, bf16[12,288,128]{2,1,0:T(8,128)(2,1)S(1)}, u32[]{:S(2)}, u32[]{:S(2)}) collective-permute-start(bf16[12,288,128]{2,1,0:T(8,128)(2,1)S(1)} %get-tuple-element.10), channel_id=1, source_target_pairs={{1,0},{2,1},{3,2},{4,3},{5,4},{6,5},{7,6},{8,7},{9,8},{10,9},{11,1... | collective-permute-start | bytes 2654216 | tf_op jit(solution)/shard_map/ppermute | solution.py:168
  130.9 34.8 %collective-permute-start.5 = (bf16[12,288,128]{2,1,0:T(8,128)(2,1)S(1)}, bf16[12,288,128]{2,1,0:T(8,128)(2,1)S(1)}, u32[]{:S(2)}, u32[]{:S(2)}) collective-permute-start(bf16[12,288,128]{2,1,0:T(8,128)(2,1)S(1)} %slice.76), channel_id=1, source_target_pairs={{0,1},{1,2},{2,3},{3,4},{4,5},{5,6},{6,7},{7,8},{8,9},{9,10},{10,1... | collective-permute-start | bytes 2654216 | tf_op jit(solution)/shard_map/ppermute | solution.py:163
  141.9 34.6 %collective-permute-start.7 = (bf16[12,288,128]{2,1,0:T(8,128)(2,1)S(1)}, bf16[12,288,128]{2,1,0:T(8,128)(2,1)S(1)}, u32[]{:S(2)}, u32[]{:S(2)}) collective-permute-start(bf16[12,288,128]{2,1,0:T(8,128)(2,1)S(1)} %slice.79), channel_id=1, source_target_pairs={{0,1},{1,2},{2,3},{3,4},{4,5},{5,6},{6,7},{7,8},{8,9},{9,10},{10,1... | collective-permute-start | bytes 2654216 | tf_op jit(solution)/shard_map/ppermute | solution.py:163
  187.9 2.9 %copy-start.1 = (bf16[32,64,64]{2,1,0:T(8,128)(2,1)S(1)}, bf16[32,64,64]{2,1,0:T(8,128)(2,1)}, u32[]{:S(2)}) copy-start(bf16[32,64,64]{2,1,0:T(8,128)(2,1)} %param.6) | copy-start | bytes 786436

commit v2 on v1

--- a/solution.py
+++ b/solution.py
@@ -1,4 +1,5 @@
 import functools
+import math
 
 import jax
 import jax.numpy as jnp
@@ -40,17 +41,21 @@
     return total
 
 
-def advect_kernel(steps, first, low, high, numbers, inverse, out, staged, field, other, across_0, across_1,
-                  number, weight, operator, field_sem, number_sem, operator_sem):
+def advect_kernel(steps, places, *refs):
+    parts, (numbers, inverse, out), scratch = refs[:len(places)], refs[len(places):len(places) + 3], refs[len(places) + 3:]
+    staged, field, other, across_0, across_1, number, weight, operator, field_sem, number_sem, operator_sem = scratch
     length, rows, _ = out.shape
     computed = length + 4 * (steps - 1)
     pairs = rows // PAIR
     loads = [
-        pltpu.make_async_copy(low, staged.at[pl.ds(0, low.shape[0])], field_sem.at[0]),
-        pltpu.make_async_copy(high, staged.at[pl.ds(low.shape[0], high.shape[0])], field_sem.at[1]),
-        pltpu.make_async_copy(numbers.at[pl.ds(first, computed)], number, number_sem),
-        pltpu.make_async_copy(inverse.at[pl.ds(first, computed)], operator, operator_sem),
+        pltpu.make_async_copy(numbers, number, number_sem),
+        pltpu.make_async_copy(inverse, operator, operator_sem),
     ]
+    for index, (ref, place) in enumerate(zip(parts, places)):
+        group, start, offset = place
+        source = ref if group is None else ref.at[:, group]
+        target = staged.at[pl.ds(start, ref.shape[0]), offset] if offset is not None else staged.at[pl.ds(start, ref.shape[0])]
+        loads.append(pltpu.make_async_copy(source, target, field_sem.at[index]))
     for load in loads:
         load.start()
     for load in loads:
@@ -72,7 +77,11 @@
                     weight[column, k, pl.ds(LEVELS, 8), :] = w
 
     def widen(column):
-        field[column] = staged[column].astype(jnp.float32)
+        if len(staged.shape) == 4:
+            held = staged[column // 2, column % 2]
+        else:
+            held = staged[column]
+        field[column] = held.astype(jnp.float32)
 
     def stencils(source, column, w_column, across):
         def lat_part(at, along, w):
@@ -129,33 +138,33 @@
         vertical(across_1, target, columns - 1, shift + columns - 1)
 
 
-def advect(steps, first, low, high, numbers, inverse):
-    rows, lanes = low.shape[1:]
-    wide = low.shape[0] + high.shape[0]
+def advect(steps, rows, staged_shape, places, parts, numbers, inverse):
+    lanes = staged_shape[-1]
+    wide = math.prod(staged_shape[:-2])
     length, computed = wide - 4 * steps, wide - 4
     anywhere = pl.BlockSpec(memory_space=pl.ANY)
     work = (length + 2 * steps) * steps * rows * lanes
     return pl.pallas_call(
-        functools.partial(advect_kernel, steps, first),
-        out_shape=jax.ShapeDtypeStruct((length, rows, lanes), low.dtype),
-        in_specs=[anywhere] * 4,
+        functools.partial(advect_kernel, steps, places),
+        out_shape=jax.ShapeDtypeStruct((length, rows, lanes), jnp.bfloat16),
+        in_specs=[anywhere] * (len(parts) + 2),
         out_specs=pl.BlockSpec(memory_space=pltpu.VMEM),
         scratch_shapes=[
-            pltpu.VMEM((wide, rows, lanes), jnp.bfloat16),
+            pltpu.VMEM(staged_shape, jnp.bfloat16),
             pltpu.VMEM((wide, rows, lanes), jnp.float32),
             pltpu.VMEM((wide, rows, lanes), jnp.float32),
             pltpu.VMEM((rows, lanes), jnp.bfloat16),
             pltpu.VMEM((rows, lanes), jnp.bfloat16),
-            pltpu.VMEM((computed,) + numbers.shape[1:], jnp.float32),
+            pltpu.VMEM(numbers.shape, jnp.float32),
             pltpu.VMEM((computed, 10, LEVELS + 8, lanes), jnp.float32),
-            pltpu.VMEM((computed,) + inverse.shape[1:], jnp.bfloat16),
-            pltpu.SemaphoreType.DMA((2,)),
+            pltpu.VMEM(inverse.shape, jnp.bfloat16),
+            pltpu.SemaphoreType.DMA((len(parts),)),
             pltpu.SemaphoreType.DMA,
             pltpu.SemaphoreType.DMA,
         ],
         compiler_params=pltpu.CompilerParams(vmem_limit_bytes=36 * 1024 * 1024),
-        cost_estimate=pl.CostEstimate(flops=work * (2 * LEVELS + 20), bytes_accessed=numbers.size * 4, transcendentals=0),
-    )(low, high, numbers, inverse)
+        cost_estimate=pl.CostEstimate(flops=work * 30 * (2 * LEVELS + 20), bytes_accessed=numbers.size * 4, transcendentals=0),
+    )(*parts, numbers, inverse)
 
 
 def from_below(array, width):
@@ -166,37 +175,59 @@
 def from_above(array, width):
     peers = lax.axis_size("tile")
     return lax.ppermute(array[:width], "tile", [((i + 1) % peers, i) for i in range(peers)])
+
+
+def twice(inverse):
+    empty = jnp.zeros_like(inverse)
+    return jnp.concatenate([jnp.concatenate([inverse, empty], 2), jnp.concatenate([empty, inverse], 2)], 1)
 
 
 def shards(ensemble, weights, patch_index, courant, vert_inverse):
     peers = lax.axis_size("mem")
     members, levels, length, lanes = ensemble.shape
     share = length // peers
+    rows = members * levels // GROUPS
     halo, shift = 4 * HALF, 2 * HALF
     below, above = shift - 2, halo - 2
 
     to_send = jnp.transpose(ensemble.reshape(members, levels, peers, share, lanes), (3, 2, 0, 1, 4))
+    to_send = [to_send[part] for part in range(share)]
+    arrived = [lax.all_to_all(to_send[0], "mem", split_axis=0, concat_axis=0, tiled=True)]
+
     patches = lax.dynamic_slice_in_dim(patch_index, lax.axis_index("mem") * share, share, 0)
-    chosen = jnp.take(weights, patches, axis=0)
-
-    arrived = [lax.all_to_all(to_send[part], "mem", split_axis=0, concat_axis=0, tiled=True) for part in range(share)]
-    tied, _ = lax.optimization_barrier(((courant, vert_inverse), to_send))
-    numbers, inverse = jnp.transpose(tied[0], (2, 0, 1, 3)), tied[1]
-    numbers = jnp.concatenate([from_below(numbers, below), numbers, from_above(numbers, above)])
-    inverse = jnp.concatenate([from_below(inverse, below), inverse, from_above(inverse, above)])
-    empty = jnp.zeros_like(inverse)
-    inverse = jnp.concatenate([jnp.concatenate([inverse, empty], 2), jnp.concatenate([empty, inverse], 2)], 1)
-
-    returned = []
+    turned = lax.optimization_barrier(jnp.swapaxes(weights, 1, 2))
+    chosen = jnp.take(turned, patches, axis=0, mode="clip")
+    numbers = jnp.transpose(courant, (2, 0, 1, 3))
+    tied, numbers_above, inverse_above, chosen = lax.optimization_barrier(
+        (to_send[1], from_above(numbers, above), from_above(vert_inverse, above), chosen))
+    arrived.append(lax.all_to_all(tied, "mem", split_axis=0, concat_axis=0, tiled=True))
+    numbers_first = jnp.concatenate([numbers[2:], numbers_above])
+    inverse_first = twice(jnp.concatenate([vert_inverse[2:], inverse_above]))
+
+    returned, sides = [], []
     for part in range(share):
-        blended = jnp.einsum("jco,clj->olj", chosen[part], arrived[part].reshape(-1, levels, lanes),
+        blended = jnp.einsum("joc,clj->olj", chosen[part], arrived[part].reshape(-1, levels, lanes),
                              preferred_element_type=jnp.float32).astype(jnp.bfloat16)
         blended = blended.reshape(arrived[part].shape)
-        returned.append(lax.all_to_all(blended, "mem", split_axis=0, concat_axis=0, tiled=True))
-    analysed = jnp.stack(returned, axis=1).reshape(length, GROUPS, -1, lanes)
-    fields = [analysed[:, group] for group in range(GROUPS)]
-    fields = [advect(HALF, below + 2, field, from_above(field, halo), numbers, inverse) for field in fields]
-    fields = [advect(HALF, 0, from_below(field, halo), field, numbers, inverse) for field in fields]
+        back = lax.all_to_all(blended, "mem", split_axis=0, concat_axis=0, tiled=True)
+        returned.append(back.reshape(peers, GROUPS, rows, lanes))
+        sides.append([from_above(returned[part][:, group], halo // share) for group in range(GROUPS)])
+
+    wide = (length + halo) // share
+    fields = []
+    for group in range(GROUPS):
+        if group == 1:
+            numbers_first, numbers_below, inverse_below = lax.optimization_barrier(
+                (numbers_first, from_below(numbers, below), from_below(vert_inverse, below)))
+        parts = returned + [sides[part][group] for part in range(share)]
+        places = [(group, 0, part) for part in range(share)] + [(None, peers, part) for part in range(share)]
+        fields.append(advect(HALF, rows, (wide, share, rows, lanes), places, parts, numbers_first, inverse_first))
+
+    numbers_last = jnp.concatenate([numbers_below, numbers, numbers_above[:below]])
+    inverse_last = twice(jnp.concatenate([inverse_below, vert_inverse, inverse_above[:below]]))
+    places = [(None, 0, None), (None, halo, None)]
+    fields = [advect(HALF, rows, (halo + length, rows, lanes), places, [from_below(field, halo), field],
+                     numbers_last, inverse_last) for field in fields]
     forecast = jnp.stack(fields, axis=1).reshape(length, members, levels, lanes)
     return jnp.transpose(forecast, (1, 2, 0, 3))
 

time: 192 us -> 174 us (0.906)
  the two profiles are of different devices: /device:TPU:193 before, /device:TPU:128 now
where the time goes in v2:
time: 174 us; the launch traced here: 172 us
  Pallas kernels  43.2 us (25%)
  local copies, waits for them, and re-layouts  41.9 us (24%)
  starting transfers between devices  36.9 us (21%)
  waiting for transfers between devices  34.3 us (20%)
  matrix products  7.88 us (5%)
  other arithmetic  7.46 us (4%)
    pallas_call x4, Pallas kernels, advect(): pl.pallas_call(functools.partial(advect_kernel, steps, places), out_shape...  43.2 us
    ppermute x4, waiting for transfers between devices, from_below(): lax.ppermute(array[array.shape[0] - width:], 'tile', [(i, (i + 1) % peers...  10.9 us
    ppermute x4, starting transfers between devices, from_below(): lax.ppermute(array[array.shape[0] - width:], 'tile', [(i, (i + 1) % peers...  10.4 us
    gather x2, local copies, waits for them, and re-layouts, shards(): chosen = jnp.take(turned, patches, axis=0, mode='clip')  9.53 us
    all_to_all x2, waiting for transfers between devices, shards(): lax.all_to_all(blended, 'mem', split_axis=0, concat_axis=0, tiled=True)  8.22 us
    dot_general x2, matrix products, shards(): jnp.einsum('joc,clj->olj', chosen[part], arrived[part].reshape(-1, levels...  7.88 us
    reshape x2, local copies, waits for them, and re-layouts, shards(): blended = blended.reshape(arrived[part].shape)  7.74 us
    ppermute x6, starting transfers between devices, from_above(): lax.ppermute(array[:width], 'tile', [((i + 1) % peers, i) for i in range(...  7.68 us
  transfers between devices with their start and end apart: 14, of which 7 were waited for; matrix products, arithmetic and copies ran while one was open for 28% of the time, Pallas kernels for 19%

profile of v2, /device:TPU:128, one launch (start us, length us, event | category | flops | bytes accessed | tf_op | source)
XLA Modules:
  0.0 171.9 jit_solution(2652178829521773152)
XLA Ops:
  0.0 2.3 %copy.36 = bf16[8,72,16,128]{3,1,2,0:T(8,128)(2,1)S(1)} copy(bf16[8,72,16,128]{3,2,1,0:T(8,128)(2,1)} %param.5) | data formatting | bytes 4718592 | tf_op args[0]
  3.7 5.3 %all-to-all-start = ((bf16[8,8,72,128]{3,2,1,0:T(8,128)(2,1)}), bf16[8,8,72,128]{3,2,1,0:T(8,128)(2,1)S(1)}, u32[]{:S(2)}, u32[]{:S(2)}) async-start(bf16[8,8,72,128]{3,2,1,0:T(8,128)(2,1)} %copy.39), calls=%async_computation | async-start | bytes 2359296 | tf_op jit(solution)/shard_map/all_to_all | solution.py:195
  9.0 1.7 copy.56
  12.7 1.6 collective-permute-start
  16.0 3.2 %gather_fusion = bf16[256,64,64]{1,2,0:T(8,128)(2,1)} fusion(bf16[32,64,64]{1,2,0:T(8,128)(2,1)S(1)} %bitcast.65, s32[1024]{0:T(1024)S(1)} %pad_clamp_fusion), kind=kCustom, calls=%fused_computation | custom fusion | bytes 4195328 | tf_op jit(solution)/shard_map/jit(_take)/gather | solution.py:199
  19.2 6.4 %copy.38 = bf16[256,64,64]{2,1,0:T(8,128)(2,1)} copy(bf16[256,64,64]{1,2,0:T(8,128)(2,1)} %gather_fusion) | data formatting | bytes 4194304 | tf_op jit(solution)/shard_map/jit(_take)/gather | solution.py:199
  25.5 3.1 %collective-permute-done.1 = bf16[10,72,72]{2,1,0:T(8,128)(2,1)S(1)} collective-permute-done((bf16[10,72,72]{2,1,0:T(8,128)(2,1)S(1)}, bf16[10,72,72]{2,1,0:T(8,128)(2,1)S(1)}, u32[]{:S(2)}, u32[]{:S(2)}) %collective-permute-start.1) | collective-permute-done | bytes 103712 | tf_op jit(solution)/shard_map/ppermute | solution.py:177
  29.8 2.0 %all-to-all-done = bf16[8,8,72,128]{3,2,1,0:T(8,128)(2,1)S(1)} async-done(((bf16[8,8,72,128]{3,2,1,0:T(8,128)(2,1)}), bf16[8,8,72,128]{3,2,1,0:T(8,128)(2,1)S(1)}, u32[]{:S(2)}, u32[]{:S(2)}) %all-to-all-start) | async-done | bytes 1179680 | tf_op jit(solution)/shard_map/all_to_all | solution.py:195
  32.8 6.3 %all-to-all-start.2 = ((bf16[8,8,72,128]{3,2,1,0:T(8,128)(2,1)}), bf16[8,8,72,128]{3,2,1,0:T(8,128)(2,1)}, u32[]{:S(2)}, u32[]{:S(2)}) async-start(bf16[8,8,72,128]{3,2,1,0:T(8,128)(2,1)} %copy.42), calls=%async_computation.2 | async-start | bytes 2359296 | tf_op jit(solution)/shard_map/all_to_all | solution.py:203
  39.1 3.1 %copy.40 = bf16[8,8,72,128]{2,1,0,3:T(8,128)(2,1)S(1)} copy(bf16[8,8,72,128]{3,2,1,0:T(8,128)(2,1)} %copy-done.6) | data formatting | bytes 2359296 | tf_op jit(solution)/shard_map/all_to_all | solution.py:195
  42.2 3.6 %convert_bitcast_fusion.1 = bf16[8,8,72,128]{2,1,0,3:T(8,128)(2,1)} fusion(bf16[8,8,72,128]{2,1,0,3:T(8,128)(2,1)S(1)} %copy.40, bf16[2,128,64,64]{3,2,1,0:T(8,128)(2,1)} %bitcast.74), kind=kOutput, calls=%fused_computation.16 | convolution fusion | flops 76087296 | bytes 4456448 | tf_op jit(solution)/shard_map/joc,clj->olj/dot_general | solution.py:209
  45.8 3.9 %copy.41 = bf16[8,8,72,128]{3,2,1,0:T(8,128)(2,1)} copy(bf16[8,8,72,128]{2,1,0,3:T(8,128)(2,1)} %convert_bitcast_fusion.1) | data formatting | bytes 2359296 | tf_op jit(solution)/shard_map/reshape | solution.py:211
  49.7 7.0 %all-to-all-done.2 = bf16[8,8,72,128]{3,2,1,0:T(8,128)(2,1)} async-done(((bf16[8,8,72,128]{3,2,1,0:T(8,128)(2,1)}), bf16[8,8,72,128]{3,2,1,0:T(8,128)(2,1)}, u32[]{:S(2)}, u32[]{:S(2)}) %all-to-all-start.2) | async-done | bytes 1179680 | tf_op jit(solution)/shard_map/all_to_all | solution.py:203
  56.7 3.6 %all-to-all-start.1 = ((bf16[8,8,72,128]{3,2,1,0:T(8,128)(2,1)}), bf16[8,8,72,128]{3,2,1,0:T(8,128)(2,1)S(1)}, u32[]{:S(2)}, u32[]{:S(2)}) async-start(bf16[8,8,72,128]{3,2,1,0:T(8,128)(2,1)} %copy.41), calls=%async_computation.1 | async-start | bytes 2359296 | tf_op jit(solution)/shard_map/all_to_all | solution.py:212
  60.2 3.7 %copy.43 = bf16[8,8,72,128]{2,1,0,3:T(8,128)(2,1)} copy(bf16[8,8,72,128]{3,2,1,0:T(8,128)(2,1)} %all-to-all-done.2) | data formatting | bytes 2359296 | tf_op jit(solution)/shard_map/all_to_all | solution.py:203
  64.0 4.3 %convert_bitcast_fusion = bf16[8,8,72,128]{2,1,0,3:T(8,128)(2,1)} fusion(bf16[2,128,64,64]{3,2,1,0:T(8,128)(2,1)} %bitcast.75, bf16[8,8,72,128]{2,1,0,3:T(8,128)(2,1)} %copy.43), kind=kOutput, calls=%fused_computation.14 | convolution fusion | flops 76087296 | bytes 5373952 | tf_op jit(solution)/shard_map/joc,clj->olj/dot_general | solution.py:209
  68.2 3.9 %copy.44 = bf16[8,8,72,128]{3,2,1,0:T(8,128)(2,1)} copy(bf16[8,8,72,128]{2,1,0,3:T(8,128)(2,1)} %convert_bitcast_fusion) | data formatting | bytes 2359296 | tf_op jit(solution)/shard_map/reshape | solution.py:211
  72.1 8.2 %all-to-all-done.1 = bf16[8,8,72,128]{3,2,1,0:T(8,128)(2,1)S(1)} async-done(((bf16[8,8,72,128]{3,2,1,0:T(8,128)(2,1)}), bf16[8,8,72,128]{3,2,1,0:T(8,128)(2,1)S(1)}, u32[]{:S(2)}, u32[]{:S(2)}) %all-to-all-start.1) | async-done | bytes 1179680 | tf_op jit(solution)/shard_map/all_to_all | solution.py:212
  80.3 3.6 %all-to-all-start.3 = ((bf16[8,8,72,128]{3,2,1,0:T(8,128)(2,1)}), bf16[8,8,72,128]{3,2,1,0:T(8,128)(2,1)S(1)}, u32[]{:S(2)}, u32[]{:S(2)}) async-start(bf16[8,8,72,128]{3,2,1,0:T(8,128)(2,1)} %copy.44), calls=%async_computation.3 | async-start | bytes 2359296 | tf_op jit(solution)/shard_map/all_to_all | solution.py:212
  85.1 4.6 %collective-permute-start.6 = (bf16[4,72,72]{2,1,0:T(8,128)(2,1)S(1)}, bf16[4,72,72]{2,1,0:T(8,128)(2,1)S(1)}, u32[]{:S(2)}, u32[]{:S(2)}) collective-permute-start(bf16[4,72,72]{2,1,0:T(8,128)(2,1)S(1)} %slice.88), channel_id=1, source_target_pairs={{0,1},{1,2},{2,3},{3,4},{4,5},{5,6},{6,7},{7,8},{8,9},{9,10},{10,1... | collective-permute-start | bytes 124424 | tf_op jit(solution)/shard_map/ppermute | solution.py:172
  91.0 2.5 %pad_maximum_fusion.1.refs_4_ = f32[24,2,72,128]{3,2,1,0:T(8,128)} fusion(f32[10,2,72,128]{3,2,1,0:T(8,128)} %collective-permute-done, f32[14,2,72,128]{3,2,1,0:T(8,128)S(1)} %slice.103), kind=kLoop, calls=%fused_computation.20 | loop fusion | flops 442368 | bytes 3538944 | tf_op jit(solution)/shard_map/concatenate | solution.py:204
  94.6 5.7 %collective-permute-done.6 = bf16[4,72,72]{2,1,0:T(8,128)(2,1)S(1)} collective-permute-done((bf16[4,72,72]{2,1,0:T(8,128)(2,1)S(1)}, bf16[4,72,72]{2,1,0:T(8,128)(2,1)S(1)}, u32[]{:S(2)}, u32[]{:S(2)}) %collective-permute-start.6) | collective-permute-done | bytes 41504 | tf_op jit(solution)/shard_map/ppermute | solution.py:172
  103.6 4.8 %collective-permute-start.3 = (bf16[6,288,128]{2,1,0:T(8,128)(2,1)S(1)}, bf16[6,288,128]{2,1,0:T(8,128)(2,1)S(1)}, u32[]{:S(2)}, u32[]{:S(2)}) collective-permute-start(bf16[6,288,128]{2,1,0:T(8,128)(2,1)S(1)} %get-tuple-element.21), channel_id=1, source_target_pairs={{1,0},{2,1},{3,2},{4,3},{5,4},{6,5},{7,6},{8,7},{9,8},{10,9},{11,1... | collective-permute-start | bytes 1327112 | tf_op jit(solution)/shard_map/ppermute | solution.py:177
  108.6 1.8 %fusion.20.refs_5_ = bf16[24,144,144]{2,1,0:T(8,128)(2,1)S(1)} fusion(bf16[24,72,72]{2,1,0:T(8,128)(2,1)} %pad_maximum_fusion.3), kind=kLoop, calls=%fused_computation.18 | loop fusion | flops 3981312 | bytes 1244160 | tf_op jit(solution)/shard_map/concatenate | solution.py:182
  111.1 3.2 %collective-permute-done.3.refs_3_ = bf16[6,288,128]{2,1,0:T(8,128)(2,1)S(1)} collective-permute-done((bf16[6,288,128]{2,1,0:T(8,128)(2,1)S(1)}, bf16[6,288,128]{2,1,0:T(8,128)(2,1)S(1)}, u32[]{:S(2)}, u32[]{:S(2)}) %collective-permute-start.3) | collective-permute-done | bytes 442400 | tf_op jit(solution)/shard_map/ppermute | solution.py:177
  114.3 10.7 %shard_map.55.refs_1_ = bf16[16,288,128]{2,1,0:T(8,128)(2,1)S(1)} custom-call(bf16[8,2,288,128]{3,2,1,0:T(8,128)(2,1)S(1)} %bitcast.67, bf16[8,2,288,128]{3,2,1,0:T(8,128)(2,1)S(1)} %bitcast.70, bf16[6,288,128]{2,1,0:T(8,128)(2,1)S(1)} %collective-permute-done.2.refs_2_, bf16[6,288,128]{2,1,0:T(8,128)(2,1)S(1)} %collective-permute-done.3.refs_3_, ...), custom_call_target="tpu_custom_call" | custom-call | flops 11970478080 | bytes 1769472 | tf_op jit(solution)/shard_map/pallas_call | solution.py:147
  125.1 5.3 %collective-permute-start.4 = (bf16[12,288,128]{2,1,0:T(8,128)(2,1)S(1)}, bf16[12,288,128]{2,1,0:T(8,128)(2,1)S(1)}, u32[]{:S(2)}, u32[]{:S(2)}) collective-permute-start(bf16[12,288,128]{2,1,0:T(8,128)(2,1)S(1)} %slice.104), channel_id=1, source_target_pairs={{0,1},{1,2},{2,3},{3,4},{4,5},{5,6},{6,7},{7,8},{8,9},{9,10},{10,1... | collective-permute-start | bytes 2654216 | tf_op jit(solution)/shard_map/ppermute | solution.py:172
  130.4 10.7 %shard_map.57.refs_1_ = bf16[16,288,128]{2,1,0:T(8,128)(2,1)S(1)} custom-call(bf16[8,2,288,128]{3,2,1,0:T(8,128)(2,1)S(1)} %bitcast.68, bf16[8,2,288,128]{3,2,1,0:T(8,128)(2,1)S(1)} %bitcast.71, bf16[6,288,128]{2,1,0:T(8,128)(2,1)S(1)} %collective-permute-done.7.refs_2_, bf16[6,288,128]{2,1,0:T(8,128)(2,1)S(1)} %collective-permute-done.8.refs_3_, ...), custom_call_target="tpu_custom_call" | custom-call | flops 11970478080 | bytes 1769472 | tf_op jit(solution)/shard_map/pallas_call | solution.py:147
  141.5 10.9 %shard_map.56 = bf16[16,288,128]{2,1,0:T(8,128)(2,1)S(1)} custom-call(bf16[12,288,128]{2,1,0:T(8,128)(2,1)S(1)} %collective-permute-done.4.refs_0_, bf16[16,288,128]{2,1,0:T(8,128)(2,1)S(1)} %shard_map.55.refs_1_, f32[24,2,72,128]{3,2,1,0:T(8,128)S(1)} %copy-done.2, bf16[24,144,144]{2,1,0:T(8,128)(2,1)S(1)} %fusion.21.refs_3_), custom_call_target="tpu_custom_call" | custom-call | flops 11970478080 | bytes 1769472 | tf_op jit(solution)/shard_map/pallas_call | solution.py:147
  152.4 5.2 %collective-permute-done.9.refs_0_ = bf16[12,288,128]{2,1,0:T(8,128)(2,1)S(1)} collective-permute-done((bf16[12,288,128]{2,1,0:T(8,128)(2,1)S(1)}, bf16[12,288,128]{2,1,0:T(8,128)(2,1)S(1)}, u32[]{:S(2)}, u32[]{:S(2)}) %collective-permute-start.9) | collective-permute-done | bytes 884768 | tf_op jit(solution)/shard_map/ppermute | solution.py:172
  157.6 10.8 %shard_map.58 = bf16[16,288,128]{2,1,0:T(8,128)(2,1)S(1)} custom-call(bf16[12,288,128]{2,1,0:T(8,128)(2,1)S(1)} %collective-permute-done.9.refs_0_, bf16[16,288,128]{2,1,0:T(8,128)(2,1)S(1)} %shard_map.57.refs_1_, f32[24,2,72,128]{3,2,1,0:T(8,128)S(1)} %copy-done.2, bf16[24,144,144]{2,1,0:T(8,128)(2,1)S(1)} %fusion.21.refs_3_), custom_call_target="tpu_custom_call" | custom-call | flops 11970478080 | bytes 1769472 | tf_op jit(solution)/shard_map/pallas_call | solution.py:147
  168.9 2.9 %copy.50 = bf16[8,72,16,128]{3,2,1,0:T(8,128)(2,1)} copy(bf16[8,72,16,128]{3,1,0,2:T(8,128)(2,1)S(1)} %bitcast.81) | data formatting | bytes 4718592 | tf_op jit(solution)/shard_map/transpose | solution.py:232
  (60 shorter events, 15.7 us)
Async XLA Ops:
  0.0 15.3 %copy-start = (bf16[32,64,64]{2,1,0:T(8,128)(2,1)S(1)}, bf16[32,64,64]{2,1,0:T(8,128)(2,1)}, u32[]{:S(2)}) copy-start(bf16[32,64,64]{2,1,0:T(8,128)(2,1)} %param.6) | copy-start | bytes 786436
  3.7 28.1 %all-to-all-start = ((bf16[8,8,72,128]{3,2,1,0:T(8,128)(2,1)}), bf16[8,8,72,128]{3,2,1,0:T(8,128)(2,1)S(1)}, u32[]{:S(2)}, u32[]{:S(2)}) async-start(bf16[8,8,72,128]{3,2,1,0:T(8,128)(2,1)} %copy.39), calls=%async_computation | async-start | bytes 2359296 | tf_op jit(solution)/shard_map/all_to_all | solution.py:195
  9.0 5.3 %copy-start.7 = (bf16[16,72,72]{2,1,0:T(8,128)(2,1)S(1)}, bf16[16,72,72]{2,1,0:T(8,128)(2,1)}, u32[]{:S(2)}) copy-start(bf16[16,72,72]{2,1,0:T(8,128)(2,1)} %param.9) | copy-start | bytes 497668
  10.7 1.0 copy-start.4
  12.7 16.0 %collective-permute-start = (f32[10,2,72,128]{3,2,1,0:T(8,128)}, f32[10,2,72,128]{3,2,1,0:T(8,128)}, u32[]{:S(2)}, u32[]{:S(2)}) collective-permute-start(f32[10,2,72,128]{3,2,1,0:T(8,128)} %slice.99), channel_id=1, source_target_pairs={{1,0},{2,1},{3,2},{4,3},{5,4},{6,5},{7,6},{8,7},{9,8},{10,9},{11,1... | collective-permute-start | bytes 2211848 | tf_op jit(solution)/shard_map/ppermute | solution.py:177
  14.3 14.3 %collective-permute-start.1 = (bf16[10,72,72]{2,1,0:T(8,128)(2,1)S(1)}, bf16[10,72,72]{2,1,0:T(8,128)(2,1)S(1)}, u32[]{:S(2)}, u32[]{:S(2)}) collective-permute-start(bf16[10,72,72]{2,1,0:T(8,128)(2,1)S(1)} %slice.76), channel_id=1, source_target_pairs={{1,0},{2,1},{3,2},{4,3},{5,4},{6,5},{7,6},{8,7},{9,8},{10,9},{11,1... | collective-permute-start | bytes 311048 | tf_op jit(solution)/shard_map/ppermute | solution.py:177
  28.6 71.6 %copy-start.10 = (bf16[10,72,72]{2,1,0:T(8,128)(2,1)}, bf16[10,72,72]{2,1,0:T(8,128)(2,1)S(1)}, u32[]{:S(2)}) copy-start(bf16[10,72,72]{2,1,0:T(8,128)(2,1)S(1)} %collective-permute-done.1) | copy-start | bytes 311044
  31.8 1.0 copy-start.6
  32.8 23.9 %all-to-all-start.2 = ((bf16[8,8,72,128]{3,2,1,0:T(8,128)(2,1)}), bf16[8,8,72,128]{3,2,1,0:T(8,128)(2,1)}, u32[]{:S(2)}, u32[]{:S(2)}) async-start(bf16[8,8,72,128]{3,2,1,0:T(8,128)(2,1)} %copy.42), calls=%async_computation.2 | async-start | bytes 2359296 | tf_op jit(solution)/shard_map/all_to_all | solution.py:203
  56.7 23.7 %all-to-all-start.1 = ((bf16[8,8,72,128]{3,2,1,0:T(8,128)(2,1)}), bf16[8,8,72,128]{3,2,1,0:T(8,128)(2,1)S(1)}, u32[]{:S(2)}, u32[]{:S(2)}) async-start(bf16[8,8,72,128]{3,2,1,0:T(8,128)(2,1)} %copy.41), calls=%async_computation.1 | async-start | bytes 2359296 | tf_op jit(solution)/shard_map/all_to_all | solution.py:212
  80.3 23.2 %all-to-all-start.3 = ((bf16[8,8,72,128]{3,2,1,0:T(8,128)(2,1)}), bf16[8,8,72,128]{3,2,1,0:T(8,128)(2,1)S(1)}, u32[]{:S(2)}, u32[]{:S(2)}) async-start(bf16[8,8,72,128]{3,2,1,0:T(8,128)(2,1)} %copy.44), calls=%async_computation.3 | async-start | bytes 2359296 | tf_op jit(solution)/shard_map/all_to_all | solution.py:212
  84.9 15.4 %collective-permute-start.5 = (f32[4,2,72,128]{3,2,1,0:T(8,128)S(1)}, f32[4,2,72,128]{3,2,1,0:T(8,128)S(1)}, u32[]{:S(2)}, u32[]{:S(2)}) collective-permute-start(f32[4,2,72,128]{3,2,1,0:T(8,128)S(1)} %slice.105), channel_id=1, source_target_pairs={{0,1},{1,2},{2,3},{3,4},{4,5},{5,6},{6,7},{7,8},{8,9},{9,10},{10,1... | collective-permute-start | bytes 884744 | tf_op jit(solution)/shard_map/ppermute | solution.py:172
  85.1 15.2 %collective-permute-start.6 = (bf16[4,72,72]{2,1,0:T(8,128)(2,1)S(1)}, bf16[4,72,72]{2,1,0:T(8,128)(2,1)S(1)}, u32[]{:S(2)}, u32[]{:S(2)}) collective-permute-start(bf16[4,72,72]{2,1,0:T(8,128)(2,1)S(1)} %slice.88), channel_id=1, source_target_pairs={{0,1},{1,2},{2,3},{3,4},{4,5},{5,6},{6,7},{7,8},{8,9},{9,10},{10,1... | collective-permute-start | bytes 124424 | tf_op jit(solution)/shard_map/ppermute | solution.py:172
  91.0 9.2 %slice-start = ((bf16[16,72,72]{2,1,0:T(8,128)(2,1)}), bf16[14,72,72]{2,1,0:T(8,128)(2,1)S(1)}, s32[]{:S(2)}) async-start(bf16[16,72,72]{2,1,0:T(8,128)(2,1)} %param.9), calls=%async_computation.4 | async-start | bytes 516096 | tf_op jit(solution)/shard_map/slice | solution.py:205
  91.0 10.1 %copy-start.5 = (f32[2,72,16,128]{3,1,0,2:T(8,128)S(1)}, f32[2,72,16,128]{3,1,0,2:T(8,128)}, u32[]{:S(2)}) copy-start(f32[2,72,16,128]{3,1,0,2:T(8,128)} %copy-done.4) | copy-start | bytes 3538948
  102.5 5.9 %copy-start.8 = (bf16[16,72,72]{2,1,0:T(8,128)(2,1)S(1)}, bf16[16,72,72]{2,1,0:T(8,128)(2,1)}, u32[]{:S(2)}) copy-start(bf16[16,72,72]{2,1,0:T(8,128)(2,1)} %param.9) | copy-start | bytes 497668
  102.5 5.9 %slice-start.1 = ((bf16[10,72,72]{2,1,0:T(8,128)(2,1)}), bf16[4,72,72]{2,1,0:T(8,128)(2,1)S(1)}, s32[]{:S(2)}) async-start(bf16[10,72,72]{2,1,0:T(8,128)(2,1)} %copy-done.10), calls=%async_computation.5 | async-start | bytes 147456 | tf_op jit(solution)/shard_map/slice | solution.py:227
  103.5 7.6 %collective-permute-start.2 = (bf16[6,288,128]{2,1,0:T(8,128)(2,1)}, bf16[6,288,128]{2,1,0:T(8,128)(2,1)S(1)}, u32[]{:S(2)}, u32[]{:S(2)}) collective-permute-start(bf16[6,288,128]{2,1,0:T(8,128)(2,1)} %get-tuple-element.23), channel_id=1, source_target_pairs={{1,0},{2,1},{3,2},{4,3},{5,4},{6,5},{7,6},{8,7},{9,8},{10,9},{11,1... | collective-permute-start | bytes 1327112 | tf_op jit(solution)/shard_map/ppermute | solution.py:177
  103.6 10.7 %collective-permute-start.3 = (bf16[6,288,128]{2,1,0:T(8,128)(2,1)S(1)}, bf16[6,288,128]{2,1,0:T(8,128)(2,1)S(1)}, u32[]{:S(2)}, u32[]{:S(2)}) collective-permute-start(bf16[6,288,128]{2,1,0:T(8,128)(2,1)S(1)} %get-tuple-element.21), channel_id=1, source_target_pairs={{1,0},{2,1},{3,2},{4,3},{5,4},{6,5},{7,6},{8,7},{9,8},{10,9},{11,1... | collective-permute-start | bytes 1327112 | tf_op jit(solution)/shard_map/ppermute | solution.py:177
  108.5 2.4 %copy-start.9 = (bf16[6,288,128]{2,1,0:T(8,128)(2,1)S(1)}, bf16[6,288,128]{2,1,0:T(8,128)(2,1)}, u32[]{:S(2)}) copy-start(bf16[6,288,128]{2,1,0:T(8,128)(2,1)} %get-tuple-element.24) | copy-start | bytes 1327108
  108.6 5.7 %copy-start.3 = (f32[24,2,72,128]{3,2,1,0:T(8,128)S(1)}, f32[24,2,72,128]{3,2,1,0:T(8,128)}, u32[]{:S(2)}) copy-start(f32[24,2,72,128]{3,2,1,0:T(8,128)} %pad_maximum_fusion.1.refs_4_) | copy-start | bytes 5308420
  110.9 19.5 %collective-permute-start.7 = (bf16[6,288,128]{2,1,0:T(8,128)(2,1)S(1)}, bf16[6,288,128]{2,1,0:T(8,128)(2,1)S(1)}, u32[]{:S(2)}, u32[]{:S(2)}) collective-permute-start(bf16[6,288,128]{2,1,0:T(8,128)(2,1)S(1)} %copy-done.9), channel_id=1, source_target_pairs={{1,0},{2,1},{3,2},{4,3},{5,4},{6,5},{7,6},{8,7},{9,8},{10,9},{11,1... | collective-permute-start | bytes 1327112 | tf_op jit(solution)/shard_map/ppermute | solution.py:177
  111.0 19.4 %collective-permute-start.8 = (bf16[6,288,128]{2,1,0:T(8,128)(2,1)S(1)}, bf16[6,288,128]{2,1,0:T(8,128)(2,1)S(1)}, u32[]{:S(2)}, u32[]{:S(2)}) collective-permute-start(bf16[6,288,128]{2,1,0:T(8,128)(2,1)S(1)} %get-tuple-element.22), channel_id=1, source_target_pairs={{1,0},{2,1},{3,2},{4,3},{5,4},{6,5},{7,6},{8,7},{9,8},{10,9},{11,1... | collective-permute-start | bytes 1327112 | tf_op jit(solution)/shard_map/ppermute | solution.py:177
  125.1 16.4 %copy-start.2 = (f32[24,2,72,128]{3,2,1,0:T(8,128)S(1)}, f32[24,2,72,128]{3,2,1,0:T(8,128)}, u32[]{:S(2)}) copy-start(f32[24,2,72,128]{3,2,1,0:T(8,128)} %pad_maximum_fusion.2.refs_2_) | copy-start | bytes 5308420
  125.1 16.4 %collective-permute-start.4 = (bf16[12,288,128]{2,1,0:T(8,128)(2,1)S(1)}, bf16[12,288,128]{2,1,0:T(8,128)(2,1)S(1)}, u32[]{:S(2)}, u32[]{:S(2)}) collective-permute-start(bf16[12,288,128]{2,1,0:T(8,128)(2,1)S(1)} %slice.104), channel_id=1, source_target_pairs={{0,1},{1,2},{2,3},{3,4},{4,5},{5,6},{6,7},{7,8},{8,9},{9,10},{10,1... | collective-permute-start | bytes 2654216 | tf_op jit(solution)/shard_map/ppermute | solution.py:172
  141.2 16.4 %collective-permute-start.9 = (bf16[12,288,128]{2,1,0:T(8,128)(2,1)S(1)}, bf16[12,288,128]{2,1,0:T(8,128)(2,1)S(1)}, u32[]{:S(2)}, u32[]{:S(2)}) collective-permute-start(bf16[12,288,128]{2,1,0:T(8,128)(2,1)S(1)} %slice.108), channel_id=1, source_target_pairs={{0,1},{1,2},{2,3},{3,4},{4,5},{5,6},{6,7},{7,8},{8,9},{9,10},{10,1... | collective-permute-start | bytes 2654216 | tf_op jit(solution)/shard_map/ppermute | solution.py:172
  168.9 2.9 %copy-start.1 = (bf16[32,64,64]{2,1,0:T(8,128)(2,1)S(1)}, bf16[32,64,64]{2,1,0:T(8,128)(2,1)}, u32[]{:S(2)}) copy-start(bf16[32,64,64]{2,1,0:T(8,128)(2,1)} %param.6) | copy-start | bytes 786436

commit v3 on v2

--- a/solution.py
+++ b/solution.py
@@ -5,6 +5,7 @@
 import jax.numpy as jnp
 from jax import lax
 from jax.experimental import pallas as pl
+from jax.experimental.layout import Layout, with_layout_constraint
 from jax.experimental.pallas import tpu as pltpu
 from jax.sharding import PartitionSpec as P
 
@@ -177,6 +178,17 @@
     return lax.ppermute(array[:width], "tile", [((i + 1) % peers, i) for i in range(peers)])
 
 
+def copied_from(step, array):
+    peers, tiles = lax.axis_size("mem"), lax.axis_size("tile")
+    pairs = []
+    for mem in range(peers):
+        for tile in range(tiles):
+            source = (tile + step) % tiles
+            holder = mem if source // 2 == tile // 2 else mem ^ 1
+            pairs.append((holder * tiles + source, mem * tiles + tile))
+    return lax.ppermute(array, ("mem", "tile"), pairs)
+
+
 def twice(inverse):
     empty = jnp.zeros_like(inverse)
     return jnp.concatenate([jnp.concatenate([inverse, empty], 2), jnp.concatenate([empty, inverse], 2)], 1)
@@ -195,32 +207,37 @@
     arrived = [lax.all_to_all(to_send[0], "mem", split_axis=0, concat_axis=0, tiled=True)]
 
     patches = lax.dynamic_slice_in_dim(patch_index, lax.axis_index("mem") * share, share, 0)
-    turned = lax.optimization_barrier(jnp.swapaxes(weights, 1, 2))
+    turned = lax.optimization_barrier(with_layout_constraint(jnp.swapaxes(weights, 1, 2), Layout((0, 1, 2))))
     chosen = jnp.take(turned, patches, axis=0, mode="clip")
     numbers = jnp.transpose(courant, (2, 0, 1, 3))
+    narrow = numbers.astype(jnp.bfloat16)
     tied, numbers_above, inverse_above, chosen = lax.optimization_barrier(
-        (to_send[1], from_above(numbers, above), from_above(vert_inverse, above), chosen))
+        (to_send[1], copied_from(1, narrow[:above]), copied_from(1, vert_inverse[:above]), chosen))
     arrived.append(lax.all_to_all(tied, "mem", split_axis=0, concat_axis=0, tiled=True))
-    numbers_first = jnp.concatenate([numbers[2:], numbers_above])
-    inverse_first = twice(jnp.concatenate([vert_inverse[2:], inverse_above]))
-
-    returned, sides = [], []
+    numbers_above = numbers_above.astype(jnp.float32)
+
+    returned = []
     for part in range(share):
         blended = jnp.einsum("joc,clj->olj", chosen[part], arrived[part].reshape(-1, levels, lanes),
                              preferred_element_type=jnp.float32).astype(jnp.bfloat16)
         blended = blended.reshape(arrived[part].shape)
+        if part == share - 1:
+            blended, numbers_below, inverse_below = lax.optimization_barrier(
+                (blended, copied_from(-1, narrow[length - below:]), copied_from(-1, vert_inverse[length - below:])))
         back = lax.all_to_all(blended, "mem", split_axis=0, concat_axis=0, tiled=True)
         returned.append(back.reshape(peers, GROUPS, rows, lanes))
-        sides.append([from_above(returned[part][:, group], halo // share) for group in range(GROUPS)])
-
+    numbers_below = numbers_below.astype(jnp.float32)
+
+    near = halo // share
+    sides = [from_above(jnp.stack([back[:near, group] for back in returned], axis=1), near) for group in range(GROUPS)]
+
+    numbers_first = jnp.concatenate([numbers[2:], numbers_above])
+    inverse_first = twice(jnp.concatenate([vert_inverse[2:], inverse_above]))
     wide = (length + halo) // share
     fields = []
     for group in range(GROUPS):
-        if group == 1:
-            numbers_first, numbers_below, inverse_below = lax.optimization_barrier(
-                (numbers_first, from_below(numbers, below), from_below(vert_inverse, below)))
-        parts = returned + [sides[part][group] for part in range(share)]
-        places = [(group, 0, part) for part in range(share)] + [(None, peers, part) for part in range(share)]
+        parts = returned + [sides[group]]
+        places = [(group, 0, 0), (group, 0, 1), (None, peers, None)]
         fields.append(advect(HALF, rows, (wide, share, rows, lanes), places, parts, numbers_first, inverse_first))
 
     numbers_last = jnp.concatenate([numbers_below, numbers, numbers_above[:below]])

time: 174 us -> 159 us (0.914)
  starting transfers between devices: 36.9 us -> 27.8 us
  local copies, waits for them, and re-layouts: 41.9 us -> 33.3 us
  waiting for transfers between devices: 34.3 us -> 39.7 us
  other arithmetic: 7.46 us -> 4.23 us
    ppermute x4 -> x2, starting transfers between devices: 10.4 us -> 0.5 us  [from_below(): lax.ppermute(array[array.shape[0] - width:], 'tile', [(i, (i + 1) % peers...]
    ppermute x0 -> x4, starting transfers between devices: none -> 6.57 us  [copied_from(): return lax.ppermute(array, ('mem', 'tile'), pairs)]
    gather x2 -> x1, local copies, waits for them, and re-layouts: 9.53 us -> 3.08 us  [shards(): chosen = jnp.take(turned, patches, axis=0, mode='clip')]
    ppermute x4 -> x2, waiting for transfers between devices: 10.9 us -> 4.95 us  [from_below(): lax.ppermute(array[array.shape[0] - width:], 'tile', [(i, (i + 1) % peers...]
    all_to_all x2, waiting for transfers between devices: 8.22 us -> 13.8 us  [shards(): lax.all_to_all(blended, 'mem', split_axis=0, concat_axis=0, tiled=True)]
    all_to_all x1, waiting for transfers between devices: 1.99 us -> 6.22 us  [shards(): lax.all_to_all(to_send[0], 'mem', split_axis=0, concat_axis=0, tiled=True)]
    reshape x2 -> x1, local copies, waits for them, and re-layouts: 7.74 us -> 3.87 us  [shards(): blended = blended.reshape(arrived[part].shape)]
    ppermute x6 -> x2, starting transfers between devices: 7.68 us -> 4.04 us  [from_above(): lax.ppermute(array[:width], 'tile', [((i + 1) % peers, i) for i in range(...]
  transfers between devices with their start and end apart: 14 -> 12, of which waited for: 7 -> 8; matrix products, arithmetic and copies ran while one was open for 28% -> 23% of each run, Pallas kernels for 19% -> 21%
where the time goes in v3:
time: 159 us; the launch traced here: 157 us
  Pallas kernels  44.7 us (28%)
  waiting for transfers between devices  39.7 us (25%)
  local copies, waits for them, and re-layouts  33.3 us (21%)
  starting transfers between devices  27.8 us (17%)
  matrix products  6.57 us (4%)
  other arithmetic  4.23 us (3%)
    pallas_call x4, Pallas kernels, advect(): pl.pallas_call(functools.partial(advect_kernel, steps, places), out_shape...  44.7 us
    all_to_all x2, waiting for transfers between devices, shards(): lax.all_to_all(blended, 'mem', split_axis=0, concat_axis=0, tiled=True)  13.8 us
    all_to_all x2, starting transfers between devices, shards(): lax.all_to_all(blended, 'mem', split_axis=0, concat_axis=0, tiled=True)  7.13 us
    ppermute x2, waiting for transfers between devices, from_above(): lax.ppermute(array[:width], 'tile', [((i + 1) % peers, i) for i in range(...  7.05 us
    all_to_all x1, waiting for transfers between devices, shards(): lax.all_to_all(tied, 'mem', split_axis=0, concat_axis=0, tiled=True)  6.68 us
    dot_general x2, matrix products, shards(): jnp.einsum('joc,clj->olj', chosen[part], arrived[part].reshape(-1, levels...  6.57 us
    ppermute x4, starting transfers between devices, copied_from(): return lax.ppermute(array, ('mem', 'tile'), pairs)  6.57 us
    all_to_all x1, waiting for transfers between devices, shards(): lax.all_to_all(to_send[0], 'mem', split_axis=0, concat_axis=0, tiled=True)  6.22 us
  transfers between devices with their start and end apart: 12, of which 8 were waited for; matrix products, arithmetic and copies ran while one was open for 23% of the time, Pallas kernels for 21%

profile of v3, /device:TPU:128, one launch (start us, length us, event | category | flops | bytes accessed | tf_op | source)
XLA Modules:
  0.0 156.7 jit_solution(17362423950662630714)
XLA Ops:
  0.0 2.3 %copy.26 = bf16[8,72,16,128]{3,1,2,0:T(8,128)(2,1)S(1)} copy(bf16[8,72,16,128]{3,2,1,0:T(8,128)(2,1)} %param.5) | data formatting | bytes 4718592 | tf_op args[0]
  3.7 5.3 %all-to-all-start = ((bf16[8,8,72,128]{3,2,1,0:T(8,128)(2,1)}), bf16[8,8,72,128]{3,2,1,0:T(8,128)(2,1)S(1)}, u32[]{:S(2)}, u32[]{:S(2)}) async-start(bf16[8,8,72,128]{3,2,1,0:T(8,128)(2,1)} %copy.29), calls=%async_computation | async-start | bytes 2359296 | tf_op jit(solution)/shard_map/all_to_all | solution.py:207
  10.3 1.9 %collective-permute-start = (bf16[10,2,72,128]{3,2,1,0:T(8,128)(2,1)}, bf16[10,2,72,128]{3,2,1,0:T(8,128)(2,1)S(1)}, u32[]{:S(2)}, u32[]{:S(2)}) collective-permute-start(bf16[10,2,72,128]{3,2,1,0:T(8,128)(2,1)} %slice.75), channel_id=1, source_target_pairs={{1,0},{34,1},{3,2},{36,3},{5,4},{38,5},{7,6},{40,7},{9,8},{42,9},{... | collective-permute-start | bytes 1105928 | tf_op jit(solution)/shard_map/ppermute | solution.py:189
  12.9 1.2 collective-permute-start.1
  14.1 1.3 copy.28
  15.5 3.1 %gather_fusion = bf16[256,64,64]{2,1,0:T(8,128)(2,1)} fusion(bf16[32,64,64]{2,1,0:T(8,128)(2,1)S(1)} %bitcast.60, s32[1024]{0:T(1024)S(1)} %pad_clamp_fusion), kind=kCustom, calls=%fused_computation | custom fusion | bytes 4195328 | tf_op jit(solution)/shard_map/jit(_take)/gather | solution.py:211
  20.7 6.2 %all-to-all-done = bf16[8,8,72,128]{3,2,1,0:T(8,128)(2,1)S(1)} async-done(((bf16[8,8,72,128]{3,2,1,0:T(8,128)(2,1)}), bf16[8,8,72,128]{3,2,1,0:T(8,128)(2,1)S(1)}, u32[]{:S(2)}, u32[]{:S(2)}) %all-to-all-start) | async-done | bytes 1179680 | tf_op jit(solution)/shard_map/all_to_all | solution.py:207
  26.9 4.3 %all-to-all-start.2 = ((bf16[8,8,72,128]{3,2,1,0:T(8,128)(2,1)}), bf16[8,8,72,128]{3,2,1,0:T(8,128)(2,1)}, u32[]{:S(2)}, u32[]{:S(2)}) async-start(bf16[8,8,72,128]{3,2,1,0:T(8,128)(2,1)} %copy.32), calls=%async_computation.2 | async-start | bytes 2359296 | tf_op jit(solution)/shard_map/all_to_all | solution.py:216
  31.2 2.3 %copy.30 = bf16[8,8,72,128]{2,1,0,3:T(8,128)(2,1)S(1)} copy(bf16[8,8,72,128]{3,2,1,0:T(8,128)(2,1)S(1)} %all-to-all-done) | data formatting | bytes 2359296 | tf_op jit(solution)/shard_map/all_to_all | solution.py:207
  33.5 3.7 %convert_bitcast_fusion.1 = bf16[8,8,72,128]{2,1,0,3:T(8,128)(2,1)} fusion(bf16[8,8,72,128]{2,1,0,3:T(8,128)(2,1)S(1)} %copy.30, bf16[2,128,64,64]{3,2,1,0:T(8,128)(2,1)} %bitcast.61), kind=kOutput, calls=%fused_computation.16 | convolution fusion | flops 76087296 | bytes 4456448 | tf_op jit(solution)/shard_map/joc,clj->olj/dot_general | solution.py:221
  37.1 3.9 %copy.31 = bf16[8,8,72,128]{3,2,1,0:T(8,128)(2,1)} copy(bf16[8,8,72,128]{2,1,0,3:T(8,128)(2,1)} %convert_bitcast_fusion.1) | data formatting | bytes 2359296 | tf_op jit(solution)/shard_map/reshape | solution.py:223
  41.0 6.7 %all-to-all-done.2 = bf16[8,8,72,128]{3,2,1,0:T(8,128)(2,1)} async-done(((bf16[8,8,72,128]{3,2,1,0:T(8,128)(2,1)}), bf16[8,8,72,128]{3,2,1,0:T(8,128)(2,1)}, u32[]{:S(2)}, u32[]{:S(2)}) %all-to-all-start.2) | async-done | bytes 1179680 | tf_op jit(solution)/shard_map/all_to_all | solution.py:216
  47.7 3.6 %all-to-all-start.1 = ((bf16[8,8,72,128]{3,2,1,0:T(8,128)(2,1)}), bf16[8,8,72,128]{3,2,1,0:T(8,128)(2,1)S(1)}, u32[]{:S(2)}, u32[]{:S(2)}) async-start(bf16[8,8,72,128]{3,2,1,0:T(8,128)(2,1)} %copy.31), calls=%async_computation.1 | async-start | bytes 2359296 | tf_op jit(solution)/shard_map/all_to_all | solution.py:227
  51.3 1.6 %slice.77 = bf16[4,2,72,128]{3,2,1,0:T(8,128)(2,1)} slice(bf16[16,2,72,128]{3,2,1,0:T(8,128)(2,1)} %bitcast.68), slice={[12:16], [0:2], [0:72], [0:128]} | slice | bytes 294912 | tf_op jit(solution)/shard_map/slice | solution.py:226
  53.5 3.5 %collective-permute-start.3 = (bf16[4,72,72]{2,1,0:T(8,128)(2,1)}, bf16[4,72,72]{2,1,0:T(8,128)(2,1)S(1)}, u32[]{:S(2)}, u32[]{:S(2)}) collective-permute-start(bf16[4,72,72]{2,1,0:T(8,128)(2,1)} %slice.61), channel_id=1, source_target_pairs={{63,0},{0,1},{33,2},{2,3},{35,4},{4,5},{37,6},{6,7},{39,8},{8,9},{... | collective-permute-start | bytes 124424 | tf_op jit(solution)/shard_map/ppermute | solution.py:189
  57.0 3.7 %copy.33 = bf16[8,8,72,128]{2,1,0,3:T(8,128)(2,1)} copy(bf16[8,8,72,128]{3,2,1,0:T(8,128)(2,1)} %all-to-all-done.2) | data formatting | bytes 2359296 | tf_op jit(solution)/shard_map/all_to_all | solution.py:216
  60.7 2.9 %convert_bitcast_fusion = bf16[8,8,72,128]{2,1,0,3:T(8,128)(2,1)S(1)} fusion(bf16[2,128,64,64]{3,2,1,0:T(8,128)(2,1)} %bitcast.62, bf16[8,8,72,128]{2,1,0,3:T(8,128)(2,1)} %copy.33), kind=kOutput, calls=%fused_computation.14 | convolution fusion | flops 76087296 | bytes 5373952 | tf_op jit(solution)/shard_map/joc,clj->olj/dot_general | solution.py:221
  63.7 2.7 %copy.34 = bf16[8,8,72,128]{3,2,1,0:T(8,128)(2,1)} copy(bf16[8,8,72,128]{2,1,0,3:T(8,128)(2,1)S(1)} %convert_bitcast_fusion) | data formatting | bytes 2359296 | tf_op jit(solution)/shard_map/optimization_barrier | solution.py:225
  67.4 3.6 %all-to-all-start.3 = ((bf16[8,8,72,128]{3,2,1,0:T(8,128)(2,1)}), bf16[8,8,72,128]{3,2,1,0:T(8,128)(2,1)S(1)}, u32[]{:S(2)}, u32[]{:S(2)}) async-start(bf16[8,8,72,128]{3,2,1,0:T(8,128)(2,1)} %copy.34), calls=%async_computation.3 | async-start | bytes 2359296 | tf_op jit(solution)/shard_map/all_to_all | solution.py:227
  70.9 1.7 %copy.40 = f32[2,72,16,128]{3,1,0,2:T(8,128)S(1)} copy(f32[2,72,16,128]{3,2,1,0:T(8,128)} %param.8) | data formatting | bytes 2359296 | tf_op args[3]
  73.5 1.3 pad_maximum_fusion.1.refs_3_
  75.8 12.8 %all-to-all-done.3 = bf16[8,8,72,128]{3,2,1,0:T(8,128)(2,1)S(1)} async-done(((bf16[8,8,72,128]{3,2,1,0:T(8,128)(2,1)}), bf16[8,8,72,128]{3,2,1,0:T(8,128)(2,1)S(1)}, u32[]{:S(2)}, u32[]{:S(2)}) %all-to-all-start.3) | async-done | bytes 1179680 | tf_op jit(solution)/shard_map/all_to_all | solution.py:227
  88.7 1.2 pad_maximum_fusion.3
  90.0 2.4 %collective-permute-start.4 = (bf16[6,2,288,128]{3,2,1,0:T(8,128)(2,1)S(1)}, bf16[6,2,288,128]{3,2,1,0:T(8,128)(2,1)S(1)}, u32[]{:S(2)}, u32[]{:S(2)}) collective-permute-start(bf16[6,2,288,128]{3,2,1,0:T(8,128)(2,1)S(1)} %pad_maximum_fusion.3), channel_id=1, source_target_pairs={{1,0},{2,1},{3,2},{4,3},{5,4},{6,5},{7,6},{8,7},{9,8},{10,9},{11,1... | collective-permute-start | bytes 2654216 | tf_op jit(solution)/shard_map/ppermute | solution.py:178
  94.3 1.6 %collective-permute-start.6 = (bf16[6,2,288,128]{3,2,1,0:T(8,128)(2,1)S(1)}, bf16[6,2,288,128]{3,2,1,0:T(8,128)(2,1)S(1)}, u32[]{:S(2)}, u32[]{:S(2)}) collective-permute-start(bf16[6,2,288,128]{3,2,1,0:T(8,128)(2,1)S(1)} %pad_maximum_fusion.4), channel_id=1, source_target_pairs={{1,0},{2,1},{3,2},{4,3},{5,4},{6,5},{7,6},{8,7},{9,8},{10,9},{11,1... | collective-permute-start | bytes 2654216 | tf_op jit(solution)/shard_map/ppermute | solution.py:178
  95.9 7.1 %collective-permute-done.4.refs_2_ = bf16[6,2,288,128]{3,2,1,0:T(8,128)(2,1)S(1)} collective-permute-done((bf16[6,2,288,128]{3,2,1,0:T(8,128)(2,1)S(1)}, bf16[6,2,288,128]{3,2,1,0:T(8,128)(2,1)S(1)}, u32[]{:S(2)}, u32[]{:S(2)}) %collective-permute-start.4) | collective-permute-done | bytes 884768 | tf_op jit(solution)/shard_map/ppermute | solution.py:178
  103.0 11.2 %shard_map.55.refs_1_ = bf16[16,288,128]{2,1,0:T(8,128)(2,1)S(1)} custom-call(bf16[8,2,288,128]{3,2,1,0:T(8,128)(2,1)S(1)} %bitcast.53, bf16[8,2,288,128]{3,2,1,0:T(8,128)(2,1)S(1)} %bitcast.56, bf16[6,2,288,128]{3,2,1,0:T(8,128)(2,1)S(1)} %collective-permute-done.4.refs_2_, f32[24,2,72,128]{3,2,1,0:T(8,128)S(1)} %copy-done.1, ...), custom_call_target="tpu_custom_call" | custom-call | flops 11970478080 | bytes 1769472 | tf_op jit(solution)/shard_map/pallas_call | solution.py:148
  114.4 11.2 %shard_map.57.refs_1_ = bf16[16,288,128]{2,1,0:T(8,128)(2,1)S(1)} custom-call(bf16[8,2,288,128]{3,2,1,0:T(8,128)(2,1)S(1)} %bitcast.54, bf16[8,2,288,128]{3,2,1,0:T(8,128)(2,1)S(1)} %bitcast.57, bf16[6,2,288,128]{3,2,1,0:T(8,128)(2,1)S(1)} %collective-permute-done.6.refs_2_, f32[24,2,72,128]{3,2,1,0:T(8,128)S(1)} %copy-done.1, ...), custom_call_target="tpu_custom_call" | custom-call | flops 11970478080 | bytes 1769472 | tf_op jit(solution)/shard_map/pallas_call | solution.py:148
  126.0 4.6 %collective-permute-done.5.refs_0_ = bf16[12,288,128]{2,1,0:T(8,128)(2,1)S(1)} collective-permute-done((bf16[12,288,128]{2,1,0:T(8,128)(2,1)S(1)}, bf16[12,288,128]{2,1,0:T(8,128)(2,1)S(1)}, u32[]{:S(2)}, u32[]{:S(2)}) %collective-permute-start.5) | collective-permute-done | bytes 884768 | tf_op jit(solution)/shard_map/ppermute | solution.py:173
  130.5 11.2 %shard_map.56 = bf16[16,288,128]{2,1,0:T(8,128)(2,1)S(1)} custom-call(bf16[12,288,128]{2,1,0:T(8,128)(2,1)S(1)} %collective-permute-done.5.refs_0_, bf16[16,288,128]{2,1,0:T(8,128)(2,1)S(1)} %shard_map.55.refs_1_, f32[24,2,72,128]{3,2,1,0:T(8,128)S(1)} %pad_maximum_fusion.2.refs_2_, bf16[24,144,144]{2,1,0:T(8,128)(2,1)S(1)} %fusion.21.refs_3_), custom_call_target="tpu_custom_call" | custom-call | flops 11970478080 | bytes 1769472 | tf_op jit(solution)/shard_map/pallas_call | solution.py:148
  142.1 11.2 %shard_map.58 = bf16[16,288,128]{2,1,0:T(8,128)(2,1)S(1)} custom-call(bf16[12,288,128]{2,1,0:T(8,128)(2,1)S(1)} %collective-permute-done.7.refs_0_, bf16[16,288,128]{2,1,0:T(8,128)(2,1)S(1)} %shard_map.57.refs_1_, f32[24,2,72,128]{3,2,1,0:T(8,128)S(1)} %pad_maximum_fusion.2.refs_2_, bf16[24,144,144]{2,1,0:T(8,128)(2,1)S(1)} %fusion.21.refs_3_), custom_call_target="tpu_custom_call" | custom-call | flops 11970478080 | bytes 1769472 | tf_op jit(solution)/shard_map/pallas_call | solution.py:148
  153.8 2.9 %copy.36 = bf16[8,72,16,128]{3,2,1,0:T(8,128)(2,1)} copy(bf16[8,72,16,128]{3,1,0,2:T(8,128)(2,1)S(1)} %bitcast.66) | data formatting | bytes 4718592 | tf_op jit(solution)/shard_map/transpose | solution.py:249
  (73 shorter events, 12.3 us)
Async XLA Ops:
  0.0 15.4 %copy-start = (s32[16,128]{1,0:T(8,128)S(1)}, s32[16,128]{1,0:T(8,128)}, u32[]{:S(2)}) copy-start(s32[16,128]{1,0:T(8,128)} %param.7) | copy-start | bytes 24580
  2.5 6.5 %copy-start.2 = (f32[2,72,16,128]{3,2,1,0:T(8,128)S(1)}, f32[2,72,16,128]{3,2,1,0:T(8,128)}, u32[]{:S(2)}) copy-start(f32[2,72,16,128]{3,2,1,0:T(8,128)} %param.8) | copy-start | bytes 3538948
  3.7 23.2 %all-to-all-start = ((bf16[8,8,72,128]{3,2,1,0:T(8,128)(2,1)}), bf16[8,8,72,128]{3,2,1,0:T(8,128)(2,1)S(1)}, u32[]{:S(2)}, u32[]{:S(2)}) async-start(bf16[8,8,72,128]{3,2,1,0:T(8,128)(2,1)} %copy.29), calls=%async_computation | async-start | bytes 2359296 | tf_op jit(solution)/shard_map/all_to_all | solution.py:207
  9.0 3.2 %copy-start.3 = (bf16[16,72,72]{2,1,0:T(8,128)(2,1)S(1)}, bf16[16,72,72]{2,1,0:T(8,128)(2,1)}, u32[]{:S(2)}) copy-start(bf16[16,72,72]{2,1,0:T(8,128)(2,1)} %param.9) | copy-start | bytes 497668
  9.4 3.5 %copy-start.6 = (bf16[2,72,16,128]{3,1,0,2:T(8,128)(2,1)}, bf16[2,72,16,128]{3,1,0,2:T(8,128)(2,1)S(1)}, u32[]{:S(2)}) copy-start(bf16[2,72,16,128]{3,1,0,2:T(8,128)(2,1)S(1)} %copy.41) | copy-start | bytes 1769476
  10.3 9.2 %collective-permute-start = (bf16[10,2,72,128]{3,2,1,0:T(8,128)(2,1)}, bf16[10,2,72,128]{3,2,1,0:T(8,128)(2,1)S(1)}, u32[]{:S(2)}, u32[]{:S(2)}) collective-permute-start(bf16[10,2,72,128]{3,2,1,0:T(8,128)(2,1)} %slice.75), channel_id=1, source_target_pairs={{1,0},{34,1},{3,2},{36,3},{5,4},{38,5},{7,6},{40,7},{9,8},{42,9},{... | collective-permute-start | bytes 1105928 | tf_op jit(solution)/shard_map/ppermute | solution.py:189
  12.9 6.6 %collective-permute-start.1 = (bf16[10,72,72]{2,1,0:T(8,128)(2,1)}, bf16[10,72,72]{2,1,0:T(8,128)(2,1)S(1)}, u32[]{:S(2)}, u32[]{:S(2)}) collective-permute-start(bf16[10,72,72]{2,1,0:T(8,128)(2,1)} %slice.56), channel_id=1, source_target_pairs={{1,0},{34,1},{3,2},{36,3},{5,4},{38,5},{7,6},{40,7},{9,8},{42,9},{... | collective-permute-start | bytes 311048 | tf_op jit(solution)/shard_map/ppermute | solution.py:189
  19.5 7.4 %copy-start.11 = (bf16[10,72,72]{2,1,0:T(8,128)(2,1)}, bf16[10,72,72]{2,1,0:T(8,128)(2,1)S(1)}, u32[]{:S(2)}) copy-start(bf16[10,72,72]{2,1,0:T(8,128)(2,1)S(1)} %collective-permute-done.1) | copy-start | bytes 311044
  19.5 7.4 %copy-start.8 = (bf16[10,2,72,128]{3,2,1,0:T(8,128)(2,1)}, bf16[10,2,72,128]{3,2,1,0:T(8,128)(2,1)S(1)}, u32[]{:S(2)}) copy-start(bf16[10,2,72,128]{3,2,1,0:T(8,128)(2,1)S(1)} %collective-permute-done) | copy-start | bytes 1105924
  26.9 20.8 %all-to-all-start.2 = ((bf16[8,8,72,128]{3,2,1,0:T(8,128)(2,1)}), bf16[8,8,72,128]{3,2,1,0:T(8,128)(2,1)}, u32[]{:S(2)}, u32[]{:S(2)}) async-start(bf16[8,8,72,128]{3,2,1,0:T(8,128)(2,1)} %copy.32), calls=%async_computation.2 | async-start | bytes 2359296 | tf_op jit(solution)/shard_map/all_to_all | solution.py:216
  41.0 11.9 %copy-start.4 = (bf16[16,72,72]{2,1,0:T(8,128)(2,1)S(1)}, bf16[16,72,72]{2,1,0:T(8,128)(2,1)}, u32[]{:S(2)}) copy-start(bf16[16,72,72]{2,1,0:T(8,128)(2,1)} %param.9) | copy-start | bytes 497668
  47.7 19.7 %all-to-all-start.1 = ((bf16[8,8,72,128]{3,2,1,0:T(8,128)(2,1)}), bf16[8,8,72,128]{3,2,1,0:T(8,128)(2,1)S(1)}, u32[]{:S(2)}, u32[]{:S(2)}) async-start(bf16[8,8,72,128]{3,2,1,0:T(8,128)(2,1)} %copy.31), calls=%async_computation.1 | async-start | bytes 2359296 | tf_op jit(solution)/shard_map/all_to_all | solution.py:227
  52.9 10.8 %collective-permute-start.2 = (bf16[4,2,72,128]{3,2,1,0:T(8,128)(2,1)}, bf16[4,2,72,128]{3,2,1,0:T(8,128)(2,1)S(1)}, u32[]{:S(2)}, u32[]{:S(2)}) collective-permute-start(bf16[4,2,72,128]{3,2,1,0:T(8,128)(2,1)} %slice.77), channel_id=1, source_target_pairs={{63,0},{0,1},{33,2},{2,3},{35,4},{4,5},{37,6},{6,7},{39,8},{8,9},{... | collective-permute-start | bytes 442376 | tf_op jit(solution)/shard_map/ppermute | solution.py:189
  53.5 10.1 %collective-permute-start.3 = (bf16[4,72,72]{2,1,0:T(8,128)(2,1)}, bf16[4,72,72]{2,1,0:T(8,128)(2,1)S(1)}, u32[]{:S(2)}, u32[]{:S(2)}) collective-permute-start(bf16[4,72,72]{2,1,0:T(8,128)(2,1)} %slice.61), channel_id=1, source_target_pairs={{63,0},{0,1},{33,2},{2,3},{35,4},{4,5},{37,6},{6,7},{39,8},{8,9},{... | collective-permute-start | bytes 124424 | tf_op jit(solution)/shard_map/ppermute | solution.py:189
  63.6 3.7 %copy-start.15 = (bf16[4,72,72]{2,1,0:T(8,128)(2,1)}, bf16[4,72,72]{2,1,0:T(8,128)(2,1)S(1)}, u32[]{:S(2)}) copy-start(bf16[4,72,72]{2,1,0:T(8,128)(2,1)S(1)} %collective-permute-done.3) | copy-start | bytes 124420
  63.6 3.7 %copy-start.13 = (bf16[4,2,72,128]{3,2,1,0:T(8,128)(2,1)}, bf16[4,2,72,128]{3,2,1,0:T(8,128)(2,1)S(1)}, u32[]{:S(2)}) copy-start(bf16[4,2,72,128]{3,2,1,0:T(8,128)(2,1)S(1)} %collective-permute-done.2) | copy-start | bytes 442372
  67.4 21.3 %all-to-all-start.3 = ((bf16[8,8,72,128]{3,2,1,0:T(8,128)(2,1)}), bf16[8,8,72,128]{3,2,1,0:T(8,128)(2,1)S(1)}, u32[]{:S(2)}, u32[]{:S(2)}) async-start(bf16[8,8,72,128]{3,2,1,0:T(8,128)(2,1)} %copy.34), calls=%async_computation.3 | async-start | bytes 2359296 | tf_op jit(solution)/shard_map/all_to_all | solution.py:227
  70.9 1.8 %copy-start.9 = (bf16[10,2,72,128]{3,2,1,0:T(8,128)(2,1)S(1)}, bf16[10,2,72,128]{3,2,1,0:T(8,128)(2,1)}, u32[]{:S(2)}) copy-start(bf16[10,2,72,128]{3,2,1,0:T(8,128)(2,1)} %copy-done.8) | copy-start | bytes 1105924
  88.6 3.8 %slice-start = ((bf16[16,72,72]{2,1,0:T(8,128)(2,1)}), bf16[14,72,72]{2,1,0:T(8,128)(2,1)S(1)}, s32[]{:S(2)}) async-start(bf16[16,72,72]{2,1,0:T(8,128)(2,1)} %param.9), calls=%async_computation.4 | async-start | bytes 516096 | tf_op jit(solution)/shard_map/slice | solution.py:235
  88.6 3.8 %copy-start.12 = (bf16[10,72,72]{2,1,0:T(8,128)(2,1)S(1)}, bf16[10,72,72]{2,1,0:T(8,128)(2,1)}, u32[]{:S(2)}) copy-start(bf16[10,72,72]{2,1,0:T(8,128)(2,1)} %copy-done.11) | copy-start | bytes 311044
  88.7 4.3 %copy-start.14 = (bf16[4,2,72,128]{3,2,1,0:T(8,128)(2,1)S(1)}, bf16[4,2,72,128]{3,2,1,0:T(8,128)(2,1)}, u32[]{:S(2)}) copy-start(bf16[4,2,72,128]{3,2,1,0:T(8,128)(2,1)} %copy-done.13) | copy-start | bytes 442372
  89.9 3.1 %copy-start.5 = (bf16[16,72,72]{2,1,0:T(8,128)(2,1)S(1)}, bf16[16,72,72]{2,1,0:T(8,128)(2,1)}, u32[]{:S(2)}) copy-start(bf16[16,72,72]{2,1,0:T(8,128)(2,1)} %param.9) | copy-start | bytes 497668
  89.9 3.1 %slice-start.1 = ((bf16[10,72,72]{2,1,0:T(8,128)(2,1)}), bf16[4,72,72]{2,1,0:T(8,128)(2,1)S(1)}, s32[]{:S(2)}) async-start(bf16[10,72,72]{2,1,0:T(8,128)(2,1)} %copy-done.11), calls=%async_computation.5 | async-start | bytes 147456 | tf_op jit(solution)/shard_map/slice | solution.py:244
  90.0 3.1 %copy-start.16 = (bf16[4,72,72]{2,1,0:T(8,128)(2,1)S(1)}, bf16[4,72,72]{2,1,0:T(8,128)(2,1)}, u32[]{:S(2)}) copy-start(bf16[4,72,72]{2,1,0:T(8,128)(2,1)} %copy-done.15) | copy-start | bytes 124420
  90.0 3.2 %copy-start.10 = (f32[4,2,72,128]{3,2,1,0:T(8,128)S(1)}, f32[4,2,72,128]{3,2,1,0:T(8,128)}, u32[]{:S(2)}) copy-start(f32[4,2,72,128]{3,2,1,0:T(8,128)} %slice.82) | copy-start | bytes 884740
  90.0 13.0 %collective-permute-start.4 = (bf16[6,2,288,128]{3,2,1,0:T(8,128)(2,1)S(1)}, bf16[6,2,288,128]{3,2,1,0:T(8,128)(2,1)S(1)}, u32[]{:S(2)}, u32[]{:S(2)}) collective-permute-start(bf16[6,2,288,128]{3,2,1,0:T(8,128)(2,1)S(1)} %pad_maximum_fusion.3), channel_id=1, source_target_pairs={{1,0},{2,1},{3,2},{4,3},{5,4},{6,5},{7,6},{8,7},{9,8},{10,9},{11,1... | collective-permute-start | bytes 2654216 | tf_op jit(solution)/shard_map/ppermute | solution.py:178
  93.2 1.0 copy-start.7
  93.3 9.6 %copy-start.1 = (f32[24,2,72,128]{3,2,1,0:T(8,128)S(1)}, f32[24,2,72,128]{3,2,1,0:T(8,128)}, u32[]{:S(2)}) copy-start(f32[24,2,72,128]{3,2,1,0:T(8,128)} %pad_maximum_fusion.1.refs_3_) | copy-start | bytes 5308420
  94.3 20.1 %collective-permute-start.6 = (bf16[6,2,288,128]{3,2,1,0:T(8,128)(2,1)S(1)}, bf16[6,2,288,128]{3,2,1,0:T(8,128)(2,1)S(1)}, u32[]{:S(2)}, u32[]{:S(2)}) collective-permute-start(bf16[6,2,288,128]{3,2,1,0:T(8,128)(2,1)S(1)} %pad_maximum_fusion.4), channel_id=1, source_target_pairs={{1,0},{2,1},{3,2},{4,3},{5,4},{6,5},{7,6},{8,7},{9,8},{10,9},{11,1... | collective-permute-start | bytes 2654216 | tf_op jit(solution)/shard_map/ppermute | solution.py:178
  114.2 16.3 %collective-permute-start.5 = (bf16[12,288,128]{2,1,0:T(8,128)(2,1)S(1)}, bf16[12,288,128]{2,1,0:T(8,128)(2,1)S(1)}, u32[]{:S(2)}, u32[]{:S(2)}) collective-permute-start(bf16[12,288,128]{2,1,0:T(8,128)(2,1)S(1)} %slice.81), channel_id=1, source_target_pairs={{0,1},{1,2},{2,3},{3,4},{4,5},{5,6},{6,7},{7,8},{8,9},{9,10},{10,1... | collective-permute-start | bytes 2654216 | tf_op jit(solution)/shard_map/ppermute | solution.py:173
  125.6 16.5 %collective-permute-start.7 = (bf16[12,288,128]{2,1,0:T(8,128)(2,1)S(1)}, bf16[12,288,128]{2,1,0:T(8,128)(2,1)S(1)}, u32[]{:S(2)}, u32[]{:S(2)}) collective-permute-start(bf16[12,288,128]{2,1,0:T(8,128)(2,1)S(1)} %slice.85), channel_id=1, source_target_pairs={{0,1},{1,2},{2,3},{3,4},{4,5},{5,6},{6,7},{7,8},{8,9},{9,10},{10,1... | collective-permute-start | bytes 2654216 | tf_op jit(solution)/shard_map/ppermute | solution.py:173

commit v4 on v3

--- a/solution.py
+++ b/solution.py
@@ -42,23 +42,28 @@
     return total
 
 
-def advect_kernel(steps, places, *refs):
-    parts, (numbers, inverse, out), scratch = refs[:len(places)], refs[len(places):len(places) + 3], refs[len(places) + 3:]
-    staged, field, other, across_0, across_1, number, weight, operator, field_sem, number_sem, operator_sem = scratch
-    length, rows, _ = out.shape
-    computed = length + 4 * (steps - 1)
+def advect_kernel(steps, places, numbers_at, mode, *refs):
+    outs = 1 if mode != "inner" else steps
+    parts, refs = refs[:len(places)], refs[len(places):]
+    borders, refs = (refs[:steps], refs[steps:]) if mode == "outer" else ((), refs)
+    (numbers, inverse, out), refs = refs[:3], refs[3:]
+    edges, scratch = refs[:outs - 1], refs[outs - 1:]
+    staged, border, field, other, across_0, across_1, number, weight, operator, field_sem, border_sem, number_sem, operator_sem = scratch
+    rows = out.shape[1]
+    computed, wide = number.shape[0], field.shape[0]
     pairs = rows // PAIR
-    loads = [
-        pltpu.make_async_copy(numbers, number, number_sem),
-        pltpu.make_async_copy(inverse, operator, operator_sem),
-    ]
+    matrices = pltpu.make_async_copy(inverse.at[pl.ds(numbers_at, computed)], operator, operator_sem)
+    loads = [pltpu.make_async_copy(numbers.at[pl.ds(numbers_at, computed)], number, number_sem)]
     for index, (ref, place) in enumerate(zip(parts, places)):
-        group, start, offset = place
-        source = ref if group is None else ref.at[:, group]
-        target = staged.at[pl.ds(start, ref.shape[0]), offset] if offset is not None else staged.at[pl.ds(start, ref.shape[0])]
+        group, begin, count, start, offset = place
+        source = ref.at[pl.ds(begin, count)] if group is None else ref.at[pl.ds(begin, count), group]
+        target = staged.at[pl.ds(start, count)] if offset is None else staged.at[pl.ds(start, count), offset]
         loads.append(pltpu.make_async_copy(source, target, field_sem.at[index]))
+    for index, ref in enumerate(borders):
+        loads.append(pltpu.make_async_copy(ref, border.at[index], border_sem.at[index]))
     for load in loads:
         load.start()
+    matrices.start()
     for load in loads:
         load.wait()
 
@@ -102,19 +107,24 @@
         side = jnp.concatenate([across[pl.ds(pair * PAIR, PAIR), :] for pair in range(pairs)], axis=1)
         mixed = jnp.dot(operator[w_column], side, preferred_element_type=jnp.float32).astype(jnp.bfloat16)
         for pair in range(pairs):
-            target[column, pl.ds(pair * PAIR, PAIR), :] = mixed[:, pair * LANES:(pair + 1) * LANES].astype(target.dtype)
+            target[column + lead, pl.ds(pair * PAIR, PAIR), :] = mixed[:, pair * LANES:(pair + 1) * LANES].astype(target.dtype)
 
     buffers = (field, other)
+    lead = 4 if mode == "outer" else 0
+    for column in range(2 * steps - 2 if lead else 0):
+        prepare(column)
     for step in range(steps):
         source = buffers[step % 2]
         target = out if step == steps - 1 else buffers[(step + 1) % 2]
-        columns = length + 4 * (steps - 1 - step)
-        shift = 2 * step
+        columns = wide - 4 if lead else wide - 4 * (step + 1)
+        shift = 2 * (steps - 1 - step) if lead else 2 * step
+        if lead:
+            target[pl.ds(0, lead)] = border[step].astype(target.dtype)
 
         def ready(column):
             if step == 0:
                 widen(column + 4)
-                prepare(column)
+                prepare(column + shift)
 
         if step == 0:
             for column in range(4):
@@ -123,6 +133,8 @@
         ready(1)
         stencils(source, 0, shift, across_0)
         stencils(source, 1, shift + 1, across_1)
+        if step == 0:
+            matrices.wait()
 
         def two_columns(index, carry):
             even = 2 * index
@@ -137,35 +149,44 @@
         lax.fori_loop(1, columns // 2, two_columns, 0)
         vertical(across_0, target, columns - 2, shift + columns - 2)
         vertical(across_1, target, columns - 1, shift + columns - 1)
-
-
-def advect(steps, rows, staged_shape, places, parts, numbers, inverse):
+        if mode == "inner" and step < steps - 1:
+            edges[step][...] = target[pl.ds(columns - 4, 4)].astype(jnp.bfloat16)
+
+
+def advect(steps, rows, staged_shape, places, parts, numbers, inverse, numbers_at=0, mode="whole", borders=()):
     lanes = staged_shape[-1]
     wide = math.prod(staged_shape[:-2])
-    length, computed = wide - 4 * steps, wide - 4
+    outer = mode == "outer"
+    length = wide if outer else wide - 4 * steps
+    computed = wide - 4 + (2 * steps - 2 if outer else 0)
     anywhere = pl.BlockSpec(memory_space=pl.ANY)
-    work = (length + 2 * steps) * steps * rows * lanes
-    return pl.pallas_call(
-        functools.partial(advect_kernel, steps, places),
-        out_shape=jax.ShapeDtypeStruct((length, rows, lanes), jnp.bfloat16),
-        in_specs=[anywhere] * (len(parts) + 2),
-        out_specs=pl.BlockSpec(memory_space=pltpu.VMEM),
+    work = (wide - 2 * steps) * steps * rows * lanes
+    out = jax.ShapeDtypeStruct((length, rows, lanes), jnp.bfloat16)
+    outs = [out] * (steps if mode == "inner" else 1)
+    given = pl.pallas_call(
+        functools.partial(advect_kernel, steps, places, numbers_at, mode),
+        out_shape=outs,
+        in_specs=[anywhere] * (len(parts) + len(borders) + 2),
+        out_specs=[pl.BlockSpec(memory_space=pltpu.VMEM)] * len(outs),
         scratch_shapes=[
             pltpu.VMEM(staged_shape, jnp.bfloat16),
+            pltpu.VMEM((steps, 4, rows, lanes) if outer else (1, 1, 16, lanes), jnp.bfloat16),
             pltpu.VMEM((wide, rows, lanes), jnp.float32),
             pltpu.VMEM((wide, rows, lanes), jnp.float32),
             pltpu.VMEM((rows, lanes), jnp.bfloat16),
             pltpu.VMEM((rows, lanes), jnp.bfloat16),
-            pltpu.VMEM(numbers.shape, jnp.float32),
+            pltpu.VMEM((computed,) + numbers.shape[1:], jnp.float32),
             pltpu.VMEM((computed, 10, LEVELS + 8, lanes), jnp.float32),
-            pltpu.VMEM(inverse.shape, jnp.bfloat16),
+            pltpu.VMEM((computed,) + inverse.shape[1:], jnp.bfloat16),
             pltpu.SemaphoreType.DMA((len(parts),)),
+            pltpu.SemaphoreType.DMA((max(1, len(borders)),)),
             pltpu.SemaphoreType.DMA,
             pltpu.SemaphoreType.DMA,
         ],
         compiler_params=pltpu.CompilerParams(vmem_limit_bytes=36 * 1024 * 1024),
         cost_estimate=pl.CostEstimate(flops=work * 30 * (2 * LEVELS + 20), bytes_accessed=numbers.size * 4, transcendentals=0),
-    )(*parts, numbers, inverse)
+    )(*parts, *borders, numbers, inverse)
+    return given if mode == "inner" else given[0]
 
 
 def from_below(array, width):
@@ -233,16 +254,17 @@
 
     numbers_first = jnp.concatenate([numbers[2:], numbers_above])
     inverse_first = twice(jnp.concatenate([vert_inverse[2:], inverse_above]))
-    wide = (length + halo) // share
     fields = []
     for group in range(GROUPS):
-        parts = returned + [sides[group]]
-        places = [(group, 0, 0), (group, 0, 1), (None, peers, None)]
-        fields.append(advect(HALF, rows, (wide, share, rows, lanes), places, parts, numbers_first, inverse_first))
+        places = [(group, 0, peers, 0, part) for part in range(share)]
+        inner = advect(HALF, rows, (peers, share, rows, lanes), places, returned, numbers_first, inverse_first, 0, "inner")
+        places = [(group, peers - 2, 2, 0, part) for part in range(share)] + [(None, 0, near, 2, None)]
+        fields.append(advect(HALF, rows, (near + 2, share, rows, lanes), places, returned + [sides[group]],
+                             numbers_first, inverse_first, 2 * HALF + 2, "outer", inner[1:] + inner[:1]))
 
     numbers_last = jnp.concatenate([numbers_below, numbers, numbers_above[:below]])
     inverse_last = twice(jnp.concatenate([inverse_below, vert_inverse, inverse_above[:below]]))
-    places = [(None, 0, None), (None, halo, None)]
+    places = [(None, 0, halo, 0, None), (None, 0, length, halo, None)]
     fields = [advect(HALF, rows, (halo + length, rows, lanes), places, [from_below(field, halo), field],
                      numbers_last, inverse_last) for field in fields]
     forecast = jnp.stack(fields, axis=1).reshape(length, members, levels, lanes)

time: 159 us -> 157 us (0.987)
  waiting for transfers between devices: 39.7 us -> 34.4 us
  Pallas kernels: 44.7 us -> 47 us
    ppermute x2, waiting for transfers between devices: 7.05 us -> 3.44 us  [from_above(): lax.ppermute(array[:width], 'tile', [((i + 1) % peers, i) for i in range(...]
    pallas_call x4 -> x6, Pallas kernels: 44.7 us -> 47 us  [advect(): pl.pallas_call(functools.partial(advect_kernel, steps, places, numbers_at...]
    all_to_all x2, waiting for transfers between devices: 13.8 us -> 12.2 us  [shards(): lax.all_to_all(blended, 'mem', split_axis=0, concat_axis=0, tiled=True)]
    unnamed x38 -> x42, local copies, waits for them, and re-layouts: 6.11 us -> 6.3 us
  transfers between devices with their start and end apart: 12 -> 12, of which waited for: 8 -> 7; matrix products, arithmetic and copies ran while one was open for 23% -> 22% of each run, Pallas kernels for 21% -> 23%
where the time goes in v4:
time: 157 us; the launch traced here: 155 us
  Pallas kernels  47 us (30%)
  waiting for transfers between devices  34.4 us (22%)
  local copies, waits for them, and re-layouts  32.1 us (20%)
  starting transfers between devices  28.8 us (18%)
  matrix products  6.56 us (4%)
  other arithmetic  5.54 us (4%)
    pallas_call x6, Pallas kernels, advect(): pl.pallas_call(functools.partial(advect_kernel, steps, places, numbers_at...  47 us
    all_to_all x2, waiting for transfers between devices, shards(): lax.all_to_all(blended, 'mem', split_axis=0, concat_axis=0, tiled=True)  12.2 us
    all_to_all x2, starting transfers between devices, shards(): lax.all_to_all(blended, 'mem', split_axis=0, concat_axis=0, tiled=True)  7.97 us
    all_to_all x1, waiting for transfers between devices, shards(): lax.all_to_all(tied, 'mem', split_axis=0, concat_axis=0, tiled=True)  6.68 us
    ppermute x4, starting transfers between devices, copied_from(): return lax.ppermute(array, ('mem', 'tile'), pairs)  6.57 us
    dot_general x2, matrix products, shards(): jnp.einsum('joc,clj->olj', chosen[part], arrived[part].reshape(-1, levels...  6.56 us
    unnamed x42, local copies, waits for them, and re-layouts  6.3 us
    all_to_all x1, waiting for transfers between devices, shards(): lax.all_to_all(to_send[0], 'mem', split_axis=0, concat_axis=0, tiled=True)  6.26 us
  transfers between devices with their start and end apart: 12, of which 7 were waited for; matrix products, arithmetic and copies ran while one was open for 22% of the time, Pallas kernels for 23%

profile of v4, /device:TPU:128, one launch (start us, length us, event | category | flops | bytes accessed | tf_op | source)
XLA Modules:
  0.0 154.7 jit_solution(9990787473878225096)
XLA Ops:
  0.0 2.3 %copy.26 = bf16[8,72,16,128]{3,1,2,0:T(8,128)(2,1)S(1)} copy(bf16[8,72,16,128]{3,2,1,0:T(8,128)(2,1)} %param.5) | data formatting | bytes 4718592 | tf_op args[0]
  3.7 5.3 %all-to-all-start = ((bf16[8,8,72,128]{3,2,1,0:T(8,128)(2,1)}), bf16[8,8,72,128]{3,2,1,0:T(8,128)(2,1)S(1)}, u32[]{:S(2)}, u32[]{:S(2)}) async-start(bf16[8,8,72,128]{3,2,1,0:T(8,128)(2,1)} %copy.29), calls=%async_computation | async-start | bytes 2359296 | tf_op jit(solution)/shard_map/all_to_all | solution.py:228
  10.2 1.9 %collective-permute-start = (bf16[10,2,72,128]{3,2,1,0:T(8,128)(2,1)}, bf16[10,2,72,128]{3,2,1,0:T(8,128)(2,1)S(1)}, u32[]{:S(2)}, u32[]{:S(2)}) collective-permute-start(bf16[10,2,72,128]{3,2,1,0:T(8,128)(2,1)} %slice.75), channel_id=1, source_target_pairs={{1,0},{34,1},{3,2},{36,3},{5,4},{38,5},{7,6},{40,7},{9,8},{42,9},{... | collective-permute-start | bytes 1105928 | tf_op jit(solution)/shard_map/ppermute | solution.py:210
  15.4 3.1 %gather_fusion = bf16[256,64,64]{2,1,0:T(8,128)(2,1)} fusion(bf16[32,64,64]{2,1,0:T(8,128)(2,1)S(1)} %bitcast.64, s32[1024]{0:T(1024)S(1)} %pad_clamp_fusion), kind=kCustom, calls=%fused_computation | custom fusion | bytes 4195328 | tf_op jit(solution)/shard_map/jit(_take)/gather | solution.py:232
  20.6 6.3 %all-to-all-done = bf16[8,8,72,128]{3,2,1,0:T(8,128)(2,1)S(1)} async-done(((bf16[8,8,72,128]{3,2,1,0:T(8,128)(2,1)}), bf16[8,8,72,128]{3,2,1,0:T(8,128)(2,1)S(1)}, u32[]{:S(2)}, u32[]{:S(2)}) %all-to-all-start) | async-done | bytes 1179680 | tf_op jit(solution)/shard_map/all_to_all | solution.py:228
  26.9 4.3 %all-to-all-start.2 = ((bf16[8,8,72,128]{3,2,1,0:T(8,128)(2,1)}), bf16[8,8,72,128]{3,2,1,0:T(8,128)(2,1)}, u32[]{:S(2)}, u32[]{:S(2)}) async-start(bf16[8,8,72,128]{3,2,1,0:T(8,128)(2,1)} %copy.32), calls=%async_computation.2 | async-start | bytes 2359296 | tf_op jit(solution)/shard_map/all_to_all | solution.py:237
  31.2 2.3 %copy.30 = bf16[8,8,72,128]{2,1,0,3:T(8,128)(2,1)S(1)} copy(bf16[8,8,72,128]{3,2,1,0:T(8,128)(2,1)S(1)} %all-to-all-done) | data formatting | bytes 2359296 | tf_op jit(solution)/shard_map/all_to_all | solution.py:228
  33.5 3.7 %convert_bitcast_fusion.1 = bf16[8,8,72,128]{2,1,0,3:T(8,128)(2,1)} fusion(bf16[8,8,72,128]{2,1,0,3:T(8,128)(2,1)S(1)} %copy.30, bf16[2,128,64,64]{3,2,1,0:T(8,128)(2,1)} %bitcast.65), kind=kOutput, calls=%fused_computation.16 | convolution fusion | flops 76087296 | bytes 4456448 | tf_op jit(solution)/shard_map/joc,clj->olj/dot_general | solution.py:242
  37.2 3.9 %copy.31 = bf16[8,8,72,128]{3,2,1,0:T(8,128)(2,1)} copy(bf16[8,8,72,128]{2,1,0,3:T(8,128)(2,1)} %convert_bitcast_fusion.1) | data formatting | bytes 2359296 | tf_op jit(solution)/shard_map/reshape | solution.py:244
  41.0 6.7 %all-to-all-done.2 = bf16[8,8,72,128]{3,2,1,0:T(8,128)(2,1)} async-done(((bf16[8,8,72,128]{3,2,1,0:T(8,128)(2,1)}), bf16[8,8,72,128]{3,2,1,0:T(8,128)(2,1)}, u32[]{:S(2)}, u32[]{:S(2)}) %all-to-all-start.2) | async-done | bytes 1179680 | tf_op jit(solution)/shard_map/all_to_all | solution.py:237
  47.7 3.6 %all-to-all-start.1 = ((bf16[8,8,72,128]{3,2,1,0:T(8,128)(2,1)}), bf16[8,8,72,128]{3,2,1,0:T(8,128)(2,1)S(1)}, u32[]{:S(2)}, u32[]{:S(2)}) async-start(bf16[8,8,72,128]{3,2,1,0:T(8,128)(2,1)} %copy.31), calls=%async_computation.1 | async-start | bytes 2359296 | tf_op jit(solution)/shard_map/all_to_all | solution.py:248
  51.3 1.6 %slice.77 = bf16[4,2,72,128]{3,2,1,0:T(8,128)(2,1)} slice(bf16[16,2,72,128]{3,2,1,0:T(8,128)(2,1)} %bitcast.72), slice={[12:16], [0:2], [0:72], [0:128]} | slice | bytes 294912 | tf_op jit(solution)/shard_map/slice | solution.py:247
  53.5 3.5 %collective-permute-start.3 = (bf16[4,72,72]{2,1,0:T(8,128)(2,1)}, bf16[4,72,72]{2,1,0:T(8,128)(2,1)S(1)}, u32[]{:S(2)}, u32[]{:S(2)}) collective-permute-start(bf16[4,72,72]{2,1,0:T(8,128)(2,1)} %slice.61), channel_id=1, source_target_pairs={{63,0},{0,1},{33,2},{2,3},{35,4},{4,5},{37,6},{6,7},{39,8},{8,9},{... | collective-permute-start | bytes 124424 | tf_op jit(solution)/shard_map/ppermute | solution.py:210
  57.0 3.7 %copy.33 = bf16[8,8,72,128]{2,1,0,3:T(8,128)(2,1)} copy(bf16[8,8,72,128]{3,2,1,0:T(8,128)(2,1)} %all-to-all-done.2) | data formatting | bytes 2359296 | tf_op jit(solution)/shard_map/all_to_all | solution.py:237
  60.7 2.9 %convert_bitcast_fusion = bf16[8,8,72,128]{2,1,0,3:T(8,128)(2,1)S(1)} fusion(bf16[2,128,64,64]{3,2,1,0:T(8,128)(2,1)} %bitcast.66, bf16[8,8,72,128]{2,1,0,3:T(8,128)(2,1)} %copy.33), kind=kOutput, calls=%fused_computation.14 | convolution fusion | flops 76087296 | bytes 5373952 | tf_op jit(solution)/shard_map/joc,clj->olj/dot_general | solution.py:242
  64.9 2.7 %copy.34 = bf16[8,8,72,128]{3,2,1,0:T(8,128)(2,1)} copy(bf16[8,8,72,128]{2,1,0,3:T(8,128)(2,1)S(1)} %convert_bitcast_fusion) | data formatting | bytes 2359296 | tf_op jit(solution)/shard_map/optimization_barrier | solution.py:246
  67.6 4.4 %all-to-all-start.3 = ((bf16[8,8,72,128]{3,2,1,0:T(8,128)(2,1)}), bf16[8,8,72,128]{3,2,1,0:T(8,128)(2,1)S(1)}, u32[]{:S(2)}, u32[]{:S(2)}) async-start(bf16[8,8,72,128]{3,2,1,0:T(8,128)(2,1)} %copy.34), calls=%async_computation.3 | async-start | bytes 2359296 | tf_op jit(solution)/shard_map/all_to_all | solution.py:248
  73.6 1.3 pad_maximum_fusion.1.refs_2_.refs_6_
  75.0 1.7 %fusion.20.refs_3_.refs_7_ = bf16[24,144,144]{2,1,0:T(8,128)(2,1)} fusion(bf16[24,72,72]{2,1,0:T(8,128)(2,1)S(1)} %pad_maximum_fusion.5), kind=kLoop, calls=%fused_computation.18 | loop fusion | flops 3981312 | bytes 1244160 | tf_op jit(solution)/shard_map/concatenate | solution.py:215
  78.1 12.2 %all-to-all-done.3 = bf16[8,8,72,128]{3,2,1,0:T(8,128)(2,1)S(1)} async-done(((bf16[8,8,72,128]{3,2,1,0:T(8,128)(2,1)}), bf16[8,8,72,128]{3,2,1,0:T(8,128)(2,1)S(1)}, u32[]{:S(2)}, u32[]{:S(2)}) %all-to-all-start.3) | async-done | bytes 1179680 | tf_op jit(solution)/shard_map/all_to_all | solution.py:248
  90.5 2.2 %collective-permute-start.4 = (bf16[6,2,288,128]{3,2,1,0:T(8,128)(2,1)S(1)}, bf16[6,2,288,128]{3,2,1,0:T(8,128)(2,1)S(1)}, u32[]{:S(2)}, u32[]{:S(2)}) collective-permute-start(bf16[6,2,288,128]{3,2,1,0:T(8,128)(2,1)S(1)} %pad_maximum_fusion.3), channel_id=1, source_target_pairs={{1,0},{2,1},{3,2},{4,3},{5,4},{6,5},{7,6},{8,7},{9,8},{10,9},{11,1... | collective-permute-start | bytes 2654216 | tf_op jit(solution)/shard_map/ppermute | solution.py:199
  93.4 1.6 %collective-permute-start.6 = (bf16[6,2,288,128]{3,2,1,0:T(8,128)(2,1)S(1)}, bf16[6,2,288,128]{3,2,1,0:T(8,128)(2,1)S(1)}, u32[]{:S(2)}, u32[]{:S(2)}) collective-permute-start(bf16[6,2,288,128]{3,2,1,0:T(8,128)(2,1)S(1)} %pad_maximum_fusion.4), channel_id=1, source_target_pairs={{1,0},{2,1},{3,2},{4,3},{5,4},{6,5},{7,6},{8,7},{9,8},{10,9},{11,1... | collective-permute-start | bytes 2654216 | tf_op jit(solution)/shard_map/ppermute | solution.py:199
  95.0 4.8 %shard_map.55 = (bf16[4,288,128]{2,1,0:T(8,128)(2,1)S(1)}, bf16[4,288,128]{2,1,0:T(8,128)(2,1)S(1)}, bf16[4,288,128]{2,1,0:T(8,128)(2,1)S(1)}) custom-call(bf16[8,2,288,128]{3,2,1,0:T(8,128)(2,1)S(1)} %bitcast.53, bf16[8,2,288,128]{3,2,1,0:T(8,128)(2,1)S(1)} %bitcast.58, f32[24,2,72,128]{3,2,1,0:T(8,128)S(1)} %copy-done.3, bf16[24,144,144]{2,1,0:T(8,128)(2,1)S(1)} %copy-done.4), custom_call_target="tpu_custom_call" | custom-call | flops 5441126400 | bytes 1769472 | tf_op jit(solution)/shard_map/pallas_call | solution.py:166
  99.8 3.4 %collective-permute-done.4.refs_2_ = bf16[6,2,288,128]{3,2,1,0:T(8,128)(2,1)S(1)} collective-permute-done((bf16[6,2,288,128]{3,2,1,0:T(8,128)(2,1)S(1)}, bf16[6,2,288,128]{3,2,1,0:T(8,128)(2,1)S(1)}, u32[]{:S(2)}, u32[]{:S(2)}) %collective-permute-start.4) | collective-permute-done | bytes 884768 | tf_op jit(solution)/shard_map/ppermute | solution.py:199
  103.2 7.5 %shard_map.56.refs_1_ = bf16[16,288,128]{2,1,0:T(8,128)(2,1)S(1)} custom-call(bf16[8,2,288,128]{3,2,1,0:T(8,128)(2,1)S(1)} %bitcast.54, bf16[8,2,288,128]{3,2,1,0:T(8,128)(2,1)S(1)} %bitcast.59, bf16[6,2,288,128]{3,2,1,0:T(8,128)(2,1)S(1)} %collective-permute-done.4.refs_2_, bf16[4,288,128]{2,1,0:T(8,128)(2,1)S(1)} %get-tuple-element.23.refs_3_, ...), custom_call_target="tpu_custom_call" | custom-call | flops 5441126400 | bytes 1769472 | tf_op jit(solution)/shard_map/pallas_call | solution.py:166
  111.3 4.8 %shard_map.58 = (bf16[4,288,128]{2,1,0:T(8,128)(2,1)S(1)}, bf16[4,288,128]{2,1,0:T(8,128)(2,1)S(1)}, bf16[4,288,128]{2,1,0:T(8,128)(2,1)S(1)}) custom-call(bf16[8,2,288,128]{3,2,1,0:T(8,128)(2,1)S(1)} %bitcast.55, bf16[8,2,288,128]{3,2,1,0:T(8,128)(2,1)S(1)} %bitcast.60, f32[24,2,72,128]{3,2,1,0:T(8,128)S(1)} %copy-done.3, bf16[24,144,144]{2,1,0:T(8,128)(2,1)S(1)} %copy-done.4), custom_call_target="tpu_custom_call" | custom-call | flops 5441126400 | bytes 1769472 | tf_op jit(solution)/shard_map/pallas_call | solution.py:166
  116.1 7.5 %shard_map.59.refs_1_ = bf16[16,288,128]{2,1,0:T(8,128)(2,1)S(1)} custom-call(bf16[8,2,288,128]{3,2,1,0:T(8,128)(2,1)S(1)} %bitcast.56, bf16[8,2,288,128]{3,2,1,0:T(8,128)(2,1)S(1)} %bitcast.61, bf16[6,2,288,128]{3,2,1,0:T(8,128)(2,1)S(1)} %collective-permute-done.6.refs_2_, bf16[4,288,128]{2,1,0:T(8,128)(2,1)S(1)} %get-tuple-element.28.refs_3_, ...), custom_call_target="tpu_custom_call" | custom-call | flops 5441126400 | bytes 1769472 | tf_op jit(solution)/shard_map/pallas_call | solution.py:166
  124.1 3.1 %collective-permute-done.5.refs_0_ = bf16[12,288,128]{2,1,0:T(8,128)(2,1)S(1)} collective-permute-done((bf16[12,288,128]{2,1,0:T(8,128)(2,1)S(1)}, bf16[12,288,128]{2,1,0:T(8,128)(2,1)S(1)}, u32[]{:S(2)}, u32[]{:S(2)}) %collective-permute-start.5) | collective-permute-done | bytes 884768 | tf_op jit(solution)/shard_map/ppermute | solution.py:194
  127.1 11.2 %shard_map.57 = bf16[16,288,128]{2,1,0:T(8,128)(2,1)S(1)} custom-call(bf16[12,288,128]{2,1,0:T(8,128)(2,1)S(1)} %collective-permute-done.5.refs_0_, bf16[16,288,128]{2,1,0:T(8,128)(2,1)S(1)} %shard_map.56.refs_1_, f32[24,2,72,128]{3,2,1,0:T(8,128)S(1)} %copy-done.2, bf16[24,144,144]{2,1,0:T(8,128)(2,1)S(1)} %fusion.21.refs_3_), custom_call_target="tpu_custom_call" | custom-call | flops 11970478080 | bytes 1769472 | tf_op jit(solution)/shard_map/pallas_call | solution.py:166
  138.3 1.8 %collective-permute-done.7.refs_0_ = bf16[12,288,128]{2,1,0:T(8,128)(2,1)S(1)} collective-permute-done((bf16[12,288,128]{2,1,0:T(8,128)(2,1)S(1)}, bf16[12,288,128]{2,1,0:T(8,128)(2,1)S(1)}, u32[]{:S(2)}, u32[]{:S(2)}) %collective-permute-start.7) | collective-permute-done | bytes 884768 | tf_op jit(solution)/shard_map/ppermute | solution.py:194
  140.1 11.2 %shard_map.60 = bf16[16,288,128]{2,1,0:T(8,128)(2,1)S(1)} custom-call(bf16[12,288,128]{2,1,0:T(8,128)(2,1)S(1)} %collective-permute-done.7.refs_0_, bf16[16,288,128]{2,1,0:T(8,128)(2,1)S(1)} %shard_map.59.refs_1_, f32[24,2,72,128]{3,2,1,0:T(8,128)S(1)} %copy-done.2, bf16[24,144,144]{2,1,0:T(8,128)(2,1)S(1)} %fusion.21.refs_3_), custom_call_target="tpu_custom_call" | custom-call | flops 11970478080 | bytes 1769472 | tf_op jit(solution)/shard_map/pallas_call | solution.py:166
  151.8 2.9 %copy.36 = bf16[8,72,16,128]{3,2,1,0:T(8,128)(2,1)} copy(bf16[8,72,16,128]{3,1,0,2:T(8,128)(2,1)S(1)} %bitcast.70) | data formatting | bytes 4718592 | tf_op jit(solution)/shard_map/transpose | solution.py:271
  (79 shorter events, 15.2 us)
Async XLA Ops:
  0.0 15.3 %copy-start = (s32[16,128]{1,0:T(8,128)S(1)}, s32[16,128]{1,0:T(8,128)}, u32[]{:S(2)}) copy-start(s32[16,128]{1,0:T(8,128)} %param.7) | copy-start | bytes 24580
  2.5 6.5 %copy-start.5 = (f32[2,72,16,128]{3,2,1,0:T(8,128)S(1)}, f32[2,72,16,128]{3,2,1,0:T(8,128)}, u32[]{:S(2)}) copy-start(f32[2,72,16,128]{3,2,1,0:T(8,128)} %param.8) | copy-start | bytes 3538948
  3.7 23.2 %all-to-all-start = ((bf16[8,8,72,128]{3,2,1,0:T(8,128)(2,1)}), bf16[8,8,72,128]{3,2,1,0:T(8,128)(2,1)S(1)}, u32[]{:S(2)}, u32[]{:S(2)}) async-start(bf16[8,8,72,128]{3,2,1,0:T(8,128)(2,1)} %copy.29), calls=%async_computation | async-start | bytes 2359296 | tf_op jit(solution)/shard_map/all_to_all | solution.py:228
  9.0 3.1 %copy-start.7 = (bf16[16,72,72]{2,1,0:T(8,128)(2,1)S(1)}, bf16[16,72,72]{2,1,0:T(8,128)(2,1)}, u32[]{:S(2)}) copy-start(bf16[16,72,72]{2,1,0:T(8,128)(2,1)} %param.9) | copy-start | bytes 497668
  9.4 3.4 %copy-start.10 = (bf16[2,72,16,128]{3,1,0,2:T(8,128)(2,1)}, bf16[2,72,16,128]{3,1,0,2:T(8,128)(2,1)S(1)}, u32[]{:S(2)}) copy-start(bf16[2,72,16,128]{3,1,0,2:T(8,128)(2,1)S(1)} %copy.41) | copy-start | bytes 1769476
  10.2 9.2 %collective-permute-start = (bf16[10,2,72,128]{3,2,1,0:T(8,128)(2,1)}, bf16[10,2,72,128]{3,2,1,0:T(8,128)(2,1)S(1)}, u32[]{:S(2)}, u32[]{:S(2)}) collective-permute-start(bf16[10,2,72,128]{3,2,1,0:T(8,128)(2,1)} %slice.75), channel_id=1, source_target_pairs={{1,0},{34,1},{3,2},{36,3},{5,4},{38,5},{7,6},{40,7},{9,8},{42,9},{... | collective-permute-start | bytes 1105928 | tf_op jit(solution)/shard_map/ppermute | solution.py:210
  12.8 6.6 %collective-permute-start.1 = (bf16[10,72,72]{2,1,0:T(8,128)(2,1)}, bf16[10,72,72]{2,1,0:T(8,128)(2,1)S(1)}, u32[]{:S(2)}, u32[]{:S(2)}) collective-permute-start(bf16[10,72,72]{2,1,0:T(8,128)(2,1)} %slice.56), channel_id=1, source_target_pairs={{1,0},{34,1},{3,2},{36,3},{5,4},{38,5},{7,6},{40,7},{9,8},{42,9},{... | collective-permute-start | bytes 311048 | tf_op jit(solution)/shard_map/ppermute | solution.py:210
  19.4 7.5 %copy-start.13 = (bf16[10,72,72]{2,1,0:T(8,128)(2,1)}, bf16[10,72,72]{2,1,0:T(8,128)(2,1)S(1)}, u32[]{:S(2)}) copy-start(bf16[10,72,72]{2,1,0:T(8,128)(2,1)S(1)} %collective-permute-done.1) | copy-start | bytes 311044
  19.4 7.5 %copy-start.11 = (bf16[10,2,72,128]{3,2,1,0:T(8,128)(2,1)}, bf16[10,2,72,128]{3,2,1,0:T(8,128)(2,1)S(1)}, u32[]{:S(2)}) copy-start(bf16[10,2,72,128]{3,2,1,0:T(8,128)(2,1)S(1)} %collective-permute-done) | copy-start | bytes 1105924
  26.9 20.8 %all-to-all-start.2 = ((bf16[8,8,72,128]{3,2,1,0:T(8,128)(2,1)}), bf16[8,8,72,128]{3,2,1,0:T(8,128)(2,1)}, u32[]{:S(2)}, u32[]{:S(2)}) async-start(bf16[8,8,72,128]{3,2,1,0:T(8,128)(2,1)} %copy.32), calls=%async_computation.2 | async-start | bytes 2359296 | tf_op jit(solution)/shard_map/all_to_all | solution.py:237
  41.0 11.8 %copy-start.8 = (bf16[16,72,72]{2,1,0:T(8,128)(2,1)S(1)}, bf16[16,72,72]{2,1,0:T(8,128)(2,1)}, u32[]{:S(2)}) copy-start(bf16[16,72,72]{2,1,0:T(8,128)(2,1)} %param.9) | copy-start | bytes 497668
  47.7 19.9 %all-to-all-start.1 = ((bf16[8,8,72,128]{3,2,1,0:T(8,128)(2,1)}), bf16[8,8,72,128]{3,2,1,0:T(8,128)(2,1)S(1)}, u32[]{:S(2)}, u32[]{:S(2)}) async-start(bf16[8,8,72,128]{3,2,1,0:T(8,128)(2,1)} %copy.31), calls=%async_computation.1 | async-start | bytes 2359296 | tf_op jit(solution)/shard_map/all_to_all | solution.py:248
  52.9 10.8 %collective-permute-start.2 = (bf16[4,2,72,128]{3,2,1,0:T(8,128)(2,1)}, bf16[4,2,72,128]{3,2,1,0:T(8,128)(2,1)S(1)}, u32[]{:S(2)}, u32[]{:S(2)}) collective-permute-start(bf16[4,2,72,128]{3,2,1,0:T(8,128)(2,1)} %slice.77), channel_id=1, source_target_pairs={{63,0},{0,1},{33,2},{2,3},{35,4},{4,5},{37,6},{6,7},{39,8},{8,9},{... | collective-permute-start | bytes 442376 | tf_op jit(solution)/shard_map/ppermute | solution.py:210
  53.5 10.1 %collective-permute-start.3 = (bf16[4,72,72]{2,1,0:T(8,128)(2,1)}, bf16[4,72,72]{2,1,0:T(8,128)(2,1)S(1)}, u32[]{:S(2)}, u32[]{:S(2)}) collective-permute-start(bf16[4,72,72]{2,1,0:T(8,128)(2,1)} %slice.61), channel_id=1, source_target_pairs={{63,0},{0,1},{33,2},{2,3},{35,4},{4,5},{37,6},{6,7},{39,8},{8,9},{... | collective-permute-start | bytes 124424 | tf_op jit(solution)/shard_map/ppermute | solution.py:210
  64.3 0.7 copy-start.15
  67.6 4.4 %copy-start.6 = (f32[2,72,16,128]{3,2,1,0:T(8,128)S(1)}, f32[2,72,16,128]{3,2,1,0:T(8,128)}, u32[]{:S(2)}) copy-start(f32[2,72,16,128]{3,2,1,0:T(8,128)} %param.8) | copy-start | bytes 3538948
  67.6 22.6 %all-to-all-start.3 = ((bf16[8,8,72,128]{3,2,1,0:T(8,128)(2,1)}), bf16[8,8,72,128]{3,2,1,0:T(8,128)(2,1)S(1)}, u32[]{:S(2)}, u32[]{:S(2)}) async-start(bf16[8,8,72,128]{3,2,1,0:T(8,128)(2,1)} %copy.34), calls=%async_computation.3 | async-start | bytes 2359296 | tf_op jit(solution)/shard_map/all_to_all | solution.py:248
  72.1 1.0 copy-start.12
  72.5 1.0 slice-start
  72.5 1.1 copy-start.14
  73.6 3.1 %copy-start.16 = (bf16[4,2,72,128]{3,2,1,0:T(8,128)(2,1)S(1)}, bf16[4,2,72,128]{3,2,1,0:T(8,128)(2,1)}, u32[]{:S(2)}) copy-start(bf16[4,2,72,128]{3,2,1,0:T(8,128)(2,1)} %copy-done.15) | copy-start | bytes 442372
  78.1 14.5 %copy-start.9 = (bf16[16,72,72]{2,1,0:T(8,128)(2,1)S(1)}, bf16[16,72,72]{2,1,0:T(8,128)(2,1)}, u32[]{:S(2)}) copy-start(bf16[16,72,72]{2,1,0:T(8,128)(2,1)} %param.9) | copy-start | bytes 497668
  90.3 2.4 %slice-start.1 = ((bf16[10,72,72]{2,1,0:T(8,128)(2,1)}), bf16[4,72,72]{2,1,0:T(8,128)(2,1)S(1)}, s32[]{:S(2)}) async-start(bf16[10,72,72]{2,1,0:T(8,128)(2,1)} %copy-done.13), calls=%async_computation.5 | async-start | bytes 147456 | tf_op jit(solution)/shard_map/slice | solution.py:266
  90.3 2.4 %copy-start.18 = (bf16[4,72,72]{2,1,0:T(8,128)(2,1)S(1)}, bf16[4,72,72]{2,1,0:T(8,128)(2,1)}, u32[]{:S(2)}) copy-start(bf16[4,72,72]{2,1,0:T(8,128)(2,1)} %copy-done.17) | copy-start | bytes 124420
  90.5 12.8 %collective-permute-start.4 = (bf16[6,2,288,128]{3,2,1,0:T(8,128)(2,1)S(1)}, bf16[6,2,288,128]{3,2,1,0:T(8,128)(2,1)S(1)}, u32[]{:S(2)}, u32[]{:S(2)}) collective-permute-start(bf16[6,2,288,128]{3,2,1,0:T(8,128)(2,1)S(1)} %pad_maximum_fusion.3), channel_id=1, source_target_pairs={{1,0},{2,1},{3,2},{4,3},{5,4},{6,5},{7,6},{8,7},{9,8},{10,9},{11,1... | collective-permute-start | bytes 2654216 | tf_op jit(solution)/shard_map/ppermute | solution.py:199
  92.8 2.2 %copy-start.3 = (f32[24,2,72,128]{3,2,1,0:T(8,128)S(1)}, f32[24,2,72,128]{3,2,1,0:T(8,128)}, u32[]{:S(2)}) copy-start(f32[24,2,72,128]{3,2,1,0:T(8,128)} %pad_maximum_fusion.1.refs_2_.refs_6_) | copy-start | bytes 5308420
  92.8 2.2 %copy-start.4 = (bf16[24,144,144]{2,1,0:T(8,128)(2,1)S(1)}, bf16[24,144,144]{2,1,0:T(8,128)(2,1)}, u32[]{:S(2)}) copy-start(bf16[24,144,144]{2,1,0:T(8,128)(2,1)} %fusion.20.refs_3_.refs_7_) | copy-start | bytes 2985988
  93.4 22.7 %collective-permute-start.6 = (bf16[6,2,288,128]{3,2,1,0:T(8,128)(2,1)S(1)}, bf16[6,2,288,128]{3,2,1,0:T(8,128)(2,1)S(1)}, u32[]{:S(2)}, u32[]{:S(2)}) collective-permute-start(bf16[6,2,288,128]{3,2,1,0:T(8,128)(2,1)S(1)} %pad_maximum_fusion.4), channel_id=1, source_target_pairs={{1,0},{2,1},{3,2},{4,3},{5,4},{6,5},{7,6},{8,7},{9,8},{10,9},{11,1... | collective-permute-start | bytes 2654216 | tf_op jit(solution)/shard_map/ppermute | solution.py:199
  110.8 16.3 %collective-permute-start.5 = (bf16[12,288,128]{2,1,0:T(8,128)(2,1)S(1)}, bf16[12,288,128]{2,1,0:T(8,128)(2,1)S(1)}, u32[]{:S(2)}, u32[]{:S(2)}) collective-permute-start(bf16[12,288,128]{2,1,0:T(8,128)(2,1)S(1)} %slice.81), channel_id=1, source_target_pairs={{0,1},{1,2},{2,3},{3,4},{4,5},{5,6},{6,7},{7,8},{8,9},{9,10},{10,1... | collective-permute-start | bytes 2654216 | tf_op jit(solution)/shard_map/ppermute | solution.py:194
  116.1 11.0 %copy-start.2 = (f32[24,2,72,128]{3,2,1,0:T(8,128)S(1)}, f32[24,2,72,128]{3,2,1,0:T(8,128)}, u32[]{:S(2)}) copy-start(f32[24,2,72,128]{3,2,1,0:T(8,128)} %pad_maximum_fusion.2.refs_2_) | copy-start | bytes 5308420
  123.8 16.4 %collective-permute-start.7 = (bf16[12,288,128]{2,1,0:T(8,128)(2,1)S(1)}, bf16[12,288,128]{2,1,0:T(8,128)(2,1)S(1)}, u32[]{:S(2)}, u32[]{:S(2)}) collective-permute-start(bf16[12,288,128]{2,1,0:T(8,128)(2,1)S(1)} %slice.85), channel_id=1, source_target_pairs={{0,1},{1,2},{2,3},{3,4},{4,5},{5,6},{6,7},{7,8},{8,9},{9,10},{10,1... | collective-permute-start | bytes 2654216 | tf_op jit(solution)/shard_map/ppermute | solution.py:194
  151.8 2.9 %copy-start.1 = (s32[16,128]{1,0:T(8,128)S(1)}, s32[16,128]{1,0:T(8,128)}, u32[]{:S(2)}) copy-start(s32[16,128]{1,0:T(8,128)} %param.7) | copy-start | bytes 24580
  (1 other events, 0.6 us)
